TPU v7x, 32 devices: a whole 2x2x4 slice. The times are simulated.
32 devices in a mesh: groups: 2 (over y), adapter: 16 (over z, x, core).
Axes of the slice: x: 2, y: 2, z: 4, core: 2. Of those that a mesh axis runs over, the one named last changes fastest.
Arguments:
- tokens: bfloat16 [1024, 8, 3200], P(('groups', 'adapter')), parts along dimension 0, may hold values from -40 to 40
- request_block_adapter: int32 [1024], P(('groups', 'adapter')), parts along dimension 0, may hold values from 0 to 127, as said below
- request_block_rows: int32 [1024], P(('groups', 'adapter')), parts along dimension 0, may hold values from 1 to 8
- adapter_down_weight: bfloat16 [128, 3200, 64], P('adapter'), may hold values from -0.109375 to 0.109375
- adapter_up_weight: bfloat16 [128, 64, 3200], P('adapter'), may hold values from -0.75 to 0.75
Outputs:
- mixed: bfloat16 [1024, 8, 3200], P(('groups', 'adapter')), parts along dimension 0
There are 2 independent parts, one for each index of `groups`. A program takes and returns all parts, laid end to end along the dimension named above; an argument that names none is the same for every part. Nothing has to cross between parts.
Inputs may be any that keep to these rules, and one draw needn't show every extreme that they name: `request_block_adapter`: adapter a is held by the device of index a // 8. The 32 blocks of one device go to at most 8 blocks for each holding device; in every draw some devices receive exactly 8 blocks from every device.
All inputs are finite; a program needn't handle non-finite values.
Results may differ from a plain program's by a relative error of at most 0.0031.
Values may be sent and summed in bfloat16 or wider, within the bound.
No kernel may reach another device: no remote copies, remote signals or barrier semaphores. Data moves between devices by JAX's collectives and lax.ppermute only.
A program may use at most 64 MiB of HBM per device.

v0:
```python
import functools

import jax
import jax.numpy as jnp
from jax import lax
from jax.experimental import pallas as pl
from jax.experimental.pallas import tpu as pltpu
from jax.sharding import PartitionSpec as P

LANES = 128
HALF = 64
QUAD = 4
VMEM = pl.BlockSpec(memory_space=pltpu.VMEM)
SMEM = pl.BlockSpec(memory_space=pltpu.SMEM)


def normalise(tokens):
    values = tokens.astype(jnp.float32)
    mean_sq = jnp.mean(values * values, axis=-1, keepdims=True)
    return (values, (values * lax.rsqrt(mean_sq + 1e-06)).astype(jnp.bfloat16))


def resident_update(hidden_state, block_labels, adapter_down_weight, adapter_up_weight):
    feature_width = hidden_state.shape[-1]
    leading = hidden_state.shape[:-1]
    resident_rows, unused_value, inner_rank = adapter_down_weight.shape
    flattened_tokens = hidden_state.reshape(-1, feature_width)
    down_matrix = jnp.einsum(
        "tq,iqg->tig", flattened_tokens, adapter_down_weight, preferred_element_type=jnp.float32
    )
    down_matrix = down_matrix.astype(jnp.bfloat16).reshape(
        flattened_tokens.shape[0], resident_rows * inner_rank
    )
    column_owner = jnp.arange(resident_rows * inner_rank, dtype=jnp.int32) // inner_rank
    picked = block_labels.reshape(-1, 1) == column_owner[None, :]
    down_matrix = jnp.where(picked, down_matrix, jnp.zeros_like(down_matrix))
    lowrank_update = jnp.dot(
        down_matrix,
        adapter_up_weight.reshape(resident_rows * inner_rank, feature_width),
        preferred_element_type=jnp.float32,
    )
    return lowrank_update.astype(jnp.bfloat16).reshape(leading + (feature_width,))


def rows_to_holders(
    tokens, request_block_adapter, request_block_rows, adapter_down_weight, adapter_up_weight
):
    blocks, rows, feature_width = tokens.shape
    devices = lax.axis_size("adapter")
    resident_rows = adapter_down_weight.shape[0]
    slots = max(1, 4 * blocks // devices)
    values, normed = normalise(tokens)
    owner = request_block_adapter // resident_rows
    within = request_block_adapter - owner * resident_rows
    serial = jnp.arange(blocks, dtype=jnp.int32)
    earlier = (owner[:, None] == owner[None, :]) & (serial[None, :] < serial[:, None])
    position = owner * slots + jnp.sum(earlier, axis=1)
    outgoing = (
        jnp.zeros((devices * slots, rows, feature_width), jnp.bfloat16).at[position].set(normed)
    )
    outgoing = outgoing.reshape(devices, slots, rows, feature_width)
    block_labels = jnp.full((devices * slots,), -1, jnp.int32).at[position].set(within)
    block_labels = jnp.broadcast_to(block_labels[:, None], (devices * slots, rows)).reshape(
        devices, slots, rows
    )
    arriving_rows, row_markers = (
        lax.all_to_all(outgoing, "adapter", split_axis=0, concat_axis=0, tiled=True),
        lax.all_to_all(block_labels, "adapter", split_axis=0, concat_axis=0, tiled=True),
    )
    lowrank_update = resident_update(
        arriving_rows, row_markers, adapter_down_weight, adapter_up_weight
    )
    returned = lax.all_to_all(lowrank_update, "adapter", split_axis=0, concat_axis=0, tiled=True)
    mine = returned.reshape(devices * slots, rows, feature_width)[position]
    live = jnp.arange(rows, dtype=jnp.int32)[None, :] < request_block_rows[:, None]
    mixed = values + jnp.where(live[:, :, None], mine.astype(jnp.float32), jnp.float32(0.0))
    return mixed.astype(jnp.bfloat16)


def lanes_of(rows):
    return lax.broadcasted_iota(jnp.int32, (rows, LANES), 1)


def weight_kernel(whole, part_ref, group_ref, weight_ref, *out_refs):
    quarter = LANES // QUAD
    inside = lanes_of(weight_ref.shape[0]) < quarter
    for k, out_ref in enumerate(out_refs):
        j = part_ref[k]
        count = out_ref.shape[0]
        start = 0 if k < 2 else pl.multiple_of(group_ref[0] * count, count)
        rows = pl.ds(start, count)
        out_ref[:, 0:whole] = weight_ref[rows, pl.ds(pl.multiple_of(j * whole, LANES), whole)]
        last = weight_ref[rows, QUAD * whole :].astype(jnp.float32)
        turned = pltpu.roll(last, lax.rem(LANES - quarter * j, LANES), 1)
        out_ref[:, whole:] = jnp.where(inside[0:count], turned, 0.0).astype(jnp.bfloat16)


def pack_kernel(whole, most_ref, target_ref, label_ref, tokens_ref, out_ref, normed_ref):
    values = tokens_ref[...].astype(jnp.float32)
    mean_sq = jnp.mean(values * values, axis=-1, keepdims=True)
    normed_ref[...] = (values * lax.rsqrt(mean_sq + 1e-06)).astype(jnp.bfloat16)
    total = tokens_ref.shape[0]
    quads, cap = out_ref.shape[0] // QUAD, out_ref.shape[1]
    quarter = LANES // QUAD
    lane = lanes_of(total)
    last = normed_ref[:, QUAD * whole :].astype(jnp.float32)
    label = jnp.where(lane == quarter, label_ref[...], 0.0)
    ends = []
    for j in range(QUAD):
        turned = pltpu.roll(last, (LANES - quarter * j) % LANES, 1) if j else last
        ends.append(jnp.where(lane < quarter, turned, label).astype(jnp.bfloat16))
    most = most_ref[0].astype(jnp.float32)
    note = jnp.where(lanes_of(cap) == quarter + 1, most, 0.0)
    for q in range(quads):
        place = lax.broadcasted_iota(jnp.int32, (cap, total), 0) + q * total
        chosen = jnp.where(target_ref[...] == place, 1.0, 0.0).astype(jnp.bfloat16)
        for j in range(QUAD):
            columns = slice(j * whole, (j + 1) * whole)
            out_ref[q * QUAD + j, :, 0:whole] = jnp.dot(
                chosen, normed_ref[:, columns], preferred_element_type=jnp.float32
            ).astype(jnp.bfloat16)
            end = jnp.dot(chosen, ends[j], preferred_element_type=jnp.float32)
            out_ref[q * QUAD + j, :, whole:] = (end + note).astype(jnp.bfloat16)


def label_of(last_tile):
    rows = last_tile.shape[0]
    quarter = LANES // QUAD
    label = last_tile[:, quarter : quarter + 1].astype(jnp.float32) - 1.0
    return label - jnp.where(lanes_of(rows) < HALF, 0.0, 1.0)


def down_kernel(first_ref, rows_ref, *refs):
    weight_refs, out_ref = refs[:-1], refs[-1]
    senders, cap, width = rows_ref.shape
    dims = (((1,), (1,)), ((), ()))
    low = lanes_of(2 * cap) < HALF

    def one(c, carry):
        rows = jnp.concatenate([rows_ref[4 * c + i] for i in range(4)], axis=0)
        label = label_of(rows[:, width - LANES :])
        picked = jnp.zeros((4 * cap, LANES), jnp.float32)
        for k, weight_ref in enumerate(weight_refs):
            product = lax.dot_general(
                rows, weight_ref[...], dims, preferred_element_type=jnp.float32
            )
            first = first_ref[k].astype(jnp.float32)
            for t in range(weight_ref.shape[0] // LANES):
                columns = slice(t * LANES, (t + 1) * LANES)
                picked = jnp.where(label == first + 2.0 * t, product[:, columns], picked)
        picked = picked + pltpu.roll(picked, HALF, 1)
        out_ref[c] = jnp.where(low, picked[0 : 2 * cap], picked[2 * cap :]).astype(jnp.bfloat16)
        return carry

    lax.fori_loop(0, senders // 4, one, 0)


def up_kernel(first_ref, rows_ref, *refs):
    sum_refs, weight_refs, out_ref = refs[:QUAD], refs[QUAD:-1], refs[-1]
    senders, cap, width = rows_ref.shape
    kept = out_ref.shape[1]
    low = lanes_of(2 * cap) < HALF

    def one(c, carry):
        down = sum_refs[0][c].astype(jnp.float32)
        for ref in sum_refs[1:]:
            down = down + ref[c].astype(jnp.float32)
        down = down.astype(jnp.bfloat16).astype(jnp.float32)
        turned = pltpu.roll(down, HALF, 1)
        pairs = [jnp.where(low, down, turned), jnp.where(low, turned, down)]
        twice = jnp.concatenate(
            [pairs[i // 2][i % 2 * cap : i % 2 * cap + kept] for i in range(4)], axis=0
        )
        ends = [rows_ref[4 * c + i, 0:kept, width - LANES :] for i in range(4)]
        label = label_of(jnp.concatenate(ends, axis=0))
        delta = jnp.zeros((4 * kept, width), jnp.float32)
        for k, weight_ref in enumerate(weight_refs):
            first = first_ref[k].astype(jnp.float32)
            placed = [
                jnp.where(label == first + 2.0 * t, twice, 0.0)
                for t in range(weight_ref.shape[0] // LANES)
            ]
            placed = jnp.concatenate(placed, axis=1).astype(jnp.bfloat16)
            delta = delta + jnp.dot(placed, weight_ref[...], preferred_element_type=jnp.float32)
        for i in range(4):
            out_ref[4 * c + i] = delta[i * kept : (i + 1) * kept].astype(jnp.bfloat16)
        return carry

    lax.fori_loop(0, senders // 4, one, 0)


def mix_kernel(whole, target_ref, tokens_ref, returned_ref, out_ref):
    total = tokens_ref.shape[0]
    quads, cap = returned_ref.shape[0] // QUAD, returned_ref.shape[1]
    quarter = LANES // QUAD
    lane = lanes_of(total)
    spot = lax.broadcasted_iota(jnp.int32, (total, quads * cap), 1)
    place = spot // cap * total + spot % cap
    chosen = jnp.where(target_ref[...] == place, 1.0, 0.0).astype(jnp.bfloat16)
    end = jnp.zeros((total, LANES), jnp.float32)
    for j in range(QUAD):
        share = jnp.concatenate([returned_ref[q * QUAD + j] for q in range(quads)], axis=0)
        delta = jnp.dot(chosen, share, preferred_element_type=jnp.float32)
        columns = slice(j * whole, (j + 1) * whole)
        out_ref[:, columns] = (
            tokens_ref[:, columns].astype(jnp.float32) + delta[:, 0:whole]
        ).astype(jnp.bfloat16)
        last = delta[:, whole:]
        turned = pltpu.roll(last, quarter * j, 1) if j else last
        end = jnp.where((lane >= quarter * j) & (lane < quarter * (j + 1)), turned, end)
    out_ref[:, QUAD * whole :] = (
        tokens_ref[:, QUAD * whole :].astype(jnp.float32) + end
    ).astype(jnp.bfloat16)


def call(kernel, out_shape, in_specs, flops, moved, after=(), scratch=()):
    many = isinstance(out_shape, list)
    skipped = len(after)
    body = (lambda *refs: kernel(*refs[skipped:])) if skipped else kernel
    run = pl.pallas_call(
        body,
        out_shape=out_shape,
        in_specs=[pl.BlockSpec(memory_space=pl.ANY)] * skipped + in_specs,
        out_specs=[VMEM] * len(out_shape) if many else VMEM,
        scratch_shapes=scratch,
        compiler_params=pltpu.CompilerParams(vmem_limit_bytes=48 * 2**20),
        cost_estimate=pl.CostEstimate(flops=flops, bytes_accessed=moved, transcendentals=0),
    )
    return functools.partial(run, *after)


def exchange(value):
    return lax.all_to_all(value, "adapter", split_axis=0, concat_axis=0, tiled=True)


def towards(value, k, devices):
    return lax.ppermute(value, "adapter", [(i, i ^ k) for i in range(devices)])


def swapped(value):
    return lax.ppermute(value, "groups", [(0, 1), (1, 0)])


def back_and_mix(
    kept, tokens, target, first, arrived, sums, up_weights, *unused_values
):
    blocks, rows, width = tokens.shape
    total = blocks * rows
    devices, cap, share = arrived.shape
    columns = sum(weight.shape[0] for weight in up_weights)
    leaving = call(
        up_kernel,
        jax.ShapeDtypeStruct((devices, kept, share), jnp.bfloat16),
        [SMEM] + [VMEM] * (1 + QUAD + len(up_weights)),
        2 * devices * kept * columns * share,
        2 * (2 * devices * kept + columns) * share,
    )(first, arrived, *sums, *up_weights)
    mixed = call(
        functools.partial(mix_kernel, share - LANES),
        jax.ShapeDtypeStruct((total, width), jnp.bfloat16),
        [VMEM] * 3,
        2 * devices * kept * total * share,
        2 * (2 * total * width + devices * kept * share),
    )(target.reshape(total, 1), tokens.reshape(total, width), exchange(leaving))
    return mixed.reshape(tokens.shape)


def start_again(tokens, target, first, arrived, sums, up_weights, *arguments):
    return rows_to_holders(tokens, *arguments)


def rows_to_quads(
    tokens, request_block_adapter, request_block_rows, adapter_down_weight, adapter_up_weight
):
    blocks, rows, width = tokens.shape
    devices = lax.axis_size("adapter")
    resident, rank, unused_width = adapter_up_weight.shape
    total = blocks * rows
    columns = resident * rank
    whole = width // LANES // QUAD * LANES
    share = whole + LANES
    bf16, i32 = jnp.bfloat16, jnp.int32

    quad = request_block_adapter // (resident * QUAD)
    label = request_block_adapter - quad * (resident * QUAD) + 1
    serial = jnp.arange(blocks, dtype=i32)
    same = quad[:, None] == quad[None, :]
    used = request_block_rows
    ahead = jnp.where(same & (serial[None, :] < serial[:, None]), used[None, :], 0)
    most = jnp.max(jnp.sum(jnp.where(same, used[None, :], 0), axis=1))
    row = jnp.arange(rows, dtype=i32)
    start = quad * total + jnp.sum(ahead, axis=1)
    target = jnp.where(row[None, :] < used[:, None], start[:, None] + row[None, :], -1)
    target = target.reshape(total).astype(i32)
    label = jnp.broadcast_to(label[:, None], (blocks, rows)).reshape(total, 1).astype(jnp.float32)

    me = lax.axis_index("adapter").astype(i32)
    group = lax.axis_index("groups").astype(i32)
    parts = jnp.bitwise_xor(me % QUAD, jnp.arange(QUAD, dtype=i32))
    own_half, twin_half = group * (resident // 2), (1 - group) * (resident // 2)
    first = jnp.concatenate(
        [parts * resident + jnp.stack([0 * group, 0 * group, own_half, own_half])]
        + [parts[2:] * resident + twin_half]
    ).astype(i32)

    def dealt(weight):
        counts = [columns, columns, columns // 2, columns // 2]
        values = call(
            functools.partial(weight_kernel, whole),
            [jax.ShapeDtypeStruct((count, share), bf16) for count in counts],
            [SMEM, SMEM, VMEM],
            0,
            4 * columns * width,
        )(parts, group.reshape(1), weight)
        near = [values[0], towards(values[1], 1, devices)]
        return near, [towards(values[k], k, devices) for k in range(2, QUAD)]

    down_near, down_far = dealt(adapter_down_weight.transpose(0, 2, 1).reshape(columns, width))
    up_near, up_far = dealt(adapter_up_weight.reshape(columns, width))
    down_weights = [*down_near, *down_far, *[swapped(value) for value in down_far]]
    up_weights = [*up_near, *up_far, *[swapped(value) for value in up_far]]

    caps = [total * 5 // 16, total * 6 // 16, total * 7 // 16]
    cap = caps[-1]
    arrived = exchange(
        call(
            functools.partial(pack_kernel, whole),
            jax.ShapeDtypeStruct((devices, cap, share), bf16),
            [SMEM, VMEM, VMEM, VMEM],
            2 * devices * cap * total * share,
            2 * (total * width + devices * cap * share),
            scratch=[pltpu.VMEM((total, width), bf16)],
        )(most.reshape(1), target.reshape(1, total), label, tokens.reshape(total, width))
    )

    most = jnp.max(arrived[:, 0, whole + LANES // QUAD + 1].astype(jnp.float32)).reshape(1, 1)
    most = jnp.maximum(most, swapped(most))[0, 0].astype(i32)
    partial = call(
        down_kernel,
        jax.ShapeDtypeStruct((devices // 4, 2 * cap, LANES), bf16),
        [SMEM] + [VMEM] * (1 + len(down_weights)),
        2 * devices * cap * 4 * columns * share,
        2 * (devices * cap + 4 * columns) * share,
        up_weights,
    )(first, arrived, *down_weights)
    sums = [partial] + [towards(partial, k, devices) for k in range(1, QUAD)]
    return lax.switch(
        sum((most > more).astype(i32) for more in caps),
        [functools.partial(back_and_mix, more) for more in caps] + [start_again],
        tokens,
        target,
        first,
        arrived,
        sums,
        up_weights,
        request_block_adapter,
        request_block_rows,
        adapter_down_weight,
        adapter_up_weight,
    )


def solution(mesh):
    placed = (
        P(("groups", "adapter"), None, None),
        P(("groups", "adapter")),
        P(("groups", "adapter")),
        P("adapter", None, None),
        P("adapter", None, None),
    )

    def per_device(tokens, request_block_adapter, request_block_rows, down_weight, up_weight):
        blocks, rows, width = tokens.shape
        devices = mesh.shape["adapter"]
        slots = max(1, 4 * blocks // devices)
        quads = devices % QUAD == 0 and slots * QUAD >= blocks
        quads = quads and width % (QUAD * LANES) == LANES and up_weight.shape[1] == HALF
        plan = rows_to_quads if quads else rows_to_holders
        return plan(tokens, request_block_adapter, request_block_rows, down_weight, up_weight)

    return jax.shard_map(
        per_device,
        mesh=mesh,
        in_specs=placed,
        out_specs=P(("groups", "adapter"), None, None),
        check_vma=False,
    )
```

profile of v0, /device:TPU:11, one launch (start us, length us, event | category | flops | bytes accessed | tf_op | source)
XLA Modules:
  0.0 234.1 jit_solution(297117562511322826)
XLA Ops:
  3.1 5.5 %shard_map.59 = bf16[16,112,896]{2,1,0:T(8,128)(2,1)} custom-call(s32[1]{0:T(128)} %bitcast.14.most_ref, s32[1,256]{1,0:T(1,128)S(1)} %select_n.72.target_ref, f32[256,1]{1,0:T(8,128)S(1)} %convert_element_type.53.label_ref, bf16[256,3200]{1,0:T(8,128)(2,1)} %bitcast.30), custom_call_target="tpu_custom_call" | custom-call | flops 822083584 | bytes 4849664 | tf_op jit(solution)/shard_map/pallas_call | solution.py:326
  8.6 6.6 %all-to-all-start.6 = ((bf16[16,112,896]{2,1,0:T(8,128)(2,1)}), bf16[16,112,896]{2,1,0:T(8,128)(2,1)}, u32[]{:S(2)}, u32[]{:S(2)}) async-start(bf16[16,112,896]{2,1,0:T(8,128)(2,1)} %shard_map.59), calls=%async_computation.6 | async-start | bytes 6422528 | tf_op jit(solution)/shard_map/all_to_all | solution.py:233
  15.2 2.2 shard_map.61
  18.0 3.1 %shard_map.60 = (bf16[512,896]{1,0:T(8,128)(2,1)}, bf16[512,896]{1,0:T(8,128)(2,1)S(1)}, bf16[256,896]{1,0:T(8,128)(2,1)S(1)}, bf16[256,896]{1,0:T(8,128)(2,1)S(1)}) custom-call(s32[4]{0:T(128)S(1)} %iota_xor_fusion.part_ref, s32[1]{0:T(128)} %bitcast.20.group_ref, bf16[512,3200]{1,0:T(8,128)(2,1)} %bitcast.36), custom_call_target="tpu_custom_call" | custom-call | bytes 6553600 | tf_op jit(solution)/shard_map/pallas_call | solution.py:308
  24.4 20.1 %collective-permute-done.8.refs_11_ = bf16[256,896]{1,0:T(8,128)(2,1)S(1)} collective-permute-done((bf16[256,896]{1,0:T(8,128)(2,1)S(1)}, bf16[256,896]{1,0:T(8,128)(2,1)S(1)}, u32[]{:S(2)}, u32[]{:S(2)}) %collective-permute-start.8) | collective-permute-done | bytes 458784 | tf_op jit(solution)/shard_map/ppermute | solution.py:237
  44.5 1.2 collective-permute-start.10
  45.7 15.0 %collective-permute-done.2.refs_2_ = bf16[256,896]{1,0:T(8,128)(2,1)} collective-permute-done((bf16[256,896]{1,0:T(8,128)(2,1)S(1)}, bf16[256,896]{1,0:T(8,128)(2,1)}, u32[]{:S(2)}, u32[]{:S(2)}) %collective-permute-start.2) | collective-permute-done | bytes 458784 | tf_op jit(solution)/shard_map/ppermute | solution.py:237
  60.7 2.6 %collective-permute-start.6 = (bf16[512,896]{1,0:T(8,128)(2,1)S(1)}, bf16[512,896]{1,0:T(8,128)(2,1)}, u32[]{:S(2)}, u32[]{:S(2)}) collective-permute-start(bf16[512,896]{1,0:T(8,128)(2,1)S(1)} %get-tuple-element.206), channel_id=1, source_target_pairs={{0,1},{1,0},{2,3},{3,2},{4,5},{5,4},{6,7},{7,6},{8,9},{9,8},{10,11... | collective-permute-start | bytes 2752520 | tf_op jit(solution)/shard_map/ppermute | solution.py:237
  63.3 13.4 %collective-permute-done.3.refs_3_ = bf16[256,896]{1,0:T(8,128)(2,1)} collective-permute-done((bf16[256,896]{1,0:T(8,128)(2,1)S(1)}, bf16[256,896]{1,0:T(8,128)(2,1)}, u32[]{:S(2)}, u32[]{:S(2)}) %collective-permute-start.3) | collective-permute-done | bytes 458784 | tf_op jit(solution)/shard_map/ppermute | solution.py:237
  76.8 1.2 collective-permute-start.4
  78.0 12.2 %collective-permute-done.7.refs_10_ = bf16[256,896]{1,0:T(8,128)(2,1)} collective-permute-done((bf16[256,896]{1,0:T(8,128)(2,1)S(1)}, bf16[256,896]{1,0:T(8,128)(2,1)}, u32[]{:S(2)}, u32[]{:S(2)}) %collective-permute-start.7) | collective-permute-done | bytes 458784 | tf_op jit(solution)/shard_map/ppermute | solution.py:237
  92.8 9.0 %collective-permute-done.5.refs_5_ = bf16[256,896]{1,0:T(8,128)(2,1)} collective-permute-done((bf16[256,896]{1,0:T(8,128)(2,1)}, bf16[256,896]{1,0:T(8,128)(2,1)}, u32[]{:S(2)}, u32[]{:S(2)}) %collective-permute-start.5) | collective-permute-done | bytes 458784 | tf_op jit(solution)/shard_map/ppermute | solution.py:241
  101.7 9.8 %collective-permute-done.9.refs_12_ = bf16[256,896]{1,0:T(8,128)(2,1)} collective-permute-done((bf16[256,896]{1,0:T(8,128)(2,1)}, bf16[256,896]{1,0:T(8,128)(2,1)}, u32[]{:S(2)}, u32[]{:S(2)}) %collective-permute-start.9) | collective-permute-done | bytes 458784 | tf_op jit(solution)/shard_map/ppermute | solution.py:241
  112.6 11.1 %shard_map.62 = bf16[4,224,128]{2,1,0:T(8,128)(2,1)S(1)} custom-call(bf16[512,896]{1,0:T(8,128)(2,1)} %get-tuple-element.201.refs_0_, bf16[512,896]{1,0:T(8,128)(2,1)} %collective-permute-done.1.refs_1_, bf16[256,896]{1,0:T(8,128)(2,1)} %collective-permute-done.2.refs_2_, bf16[256,896]{1,0:T(8,128)(2,1)} %collective-permute-done.3.refs_3_, ...), custom_call_target="tpu_custom_call" | custom-call | flops 6576668672 | bytes 6881280 | tf_op jit(solution)/shard_map/pallas_call | solution.py:338
  123.8 1.8 collective-permute-start.11
  127.3 1.5 slice_reduce_fusion
  129.4 2.0 collective-permute-start
  133.5 4.4 %collective-permute-done.13 = bf16[4,224,128]{2,1,0:T(8,128)(2,1)S(1)} collective-permute-done((bf16[4,224,128]{2,1,0:T(8,128)(2,1)S(1)}, bf16[4,224,128]{2,1,0:T(8,128)(2,1)S(1)}, u32[]{:S(2)}, u32[]{:S(2)}) %collective-permute-start.13) | collective-permute-done | bytes 229408 | tf_op jit(solution)/shard_map/ppermute | solution.py:237
  138.0 94.9 %conditional.1 = (bf16[32,8,3200]{2,1,0:T(8,128)(2,1)S(1)}) conditional(s32[]{:T(128)} %bitcast.18, (s32[32,8]{1,0:T(8,128)S(1)}, s32[32,8]{1,0:T(8,128)S(1)}, s32[32,8]{1,0:T(8,128)S(1)}, s32[32,8]{1,0:T(8,128)S(1)}, bf16[32,8,3200]{2,1,0:T(8,128)(2,1)}, /*index=5*/s32[6]{0:T(128)S(1)}, ...), branch_computations={%region_4.5_spmd, %region_5.6_spmd, %region_6.7_spmd, %region_7.12... | conditional | flops 7398753280 | bytes 120688824 | solution.py:347
  138.9 11.3 %branch_2_fun.2 = bf16[16,112,896]{2,1,0:T(8,128)(2,1)S(1)} custom-call(s32[6]{0:T(128)S(1)} %get-tuple-element.176.first_ref, bf16[16,112,896]{2,1,0:T(8,128)(2,1)} %get-tuple-element.177.rows_ref, bf16[4,224,128]{2,1,0:T(8,128)(2,1)S(1)} %get-tuple-element.178.refs_0_, bf16[4,224,128]{2,1,0:T(8,128)(2,1)S(1)} %get-tuple-element.179.refs_1_, ...), custom_call_target="tpu_custom_call" | custom-call | flops 6576668672 | bytes 10092544 | tf_op jit(solution)/shard_map/cond/branch_2_fun/pallas_call | solution.py:251
  150.2 1.6 copy-done
  151.8 6.5 %all-to-all-start.2 = ((bf16[16,112,896]{2,1,0:T(8,128)(2,1)}), bf16[16,112,896]{2,1,0:T(8,128)(2,1)S(1)}, u32[]{:S(2)}, u32[]{:S(2)}) async-start(bf16[16,112,896]{2,1,0:T(8,128)(2,1)} %copy-done), calls=%async_computation.2 | async-start | bytes 6422528 | tf_op jit(solution)/shard_map/cond/branch_2_fun/all_to_all | solution.py:233
  158.5 71.2 %all-to-all-done.2.returned_ref = bf16[16,112,896]{2,1,0:T(8,128)(2,1)S(1)} async-done(((bf16[16,112,896]{2,1,0:T(8,128)(2,1)}), bf16[16,112,896]{2,1,0:T(8,128)(2,1)S(1)}, u32[]{:S(2)}, u32[]{:S(2)}) %all-to-all-start.2) | async-done | bytes 3211296 | tf_op jit(solution)/shard_map/cond/branch_2_fun/all_to_all | solution.py:233
  229.7 2.8 %branch_2_fun.3 = bf16[256,3200]{1,0:T(8,128)(2,1)S(1)} custom-call(s32[256,1]{1,0:T(8,128)S(1)} %reshape_reshape.12.target_ref, bf16[256,3200]{1,0:T(8,128)(2,1)} %bitcast.33, bf16[16,112,896]{2,1,0:T(8,128)(2,1)S(1)} %all-to-all-done.2.returned_ref), custom_call_target="tpu_custom_call" | custom-call | flops 822083584 | bytes 6488064 | tf_op jit(solution)/shard_map/cond/branch_2_fun/pallas_call | solution.py:258
  (50 shorter events, 15.1 us)
Async XLA Ops:
  8.6 103.0 %all-to-all-start.6 = ((bf16[16,112,896]{2,1,0:T(8,128)(2,1)}), bf16[16,112,896]{2,1,0:T(8,128)(2,1)}, u32[]{:S(2)}, u32[]{:S(2)}) async-start(bf16[16,112,896]{2,1,0:T(8,128)(2,1)} %shard_map.59), calls=%async_computation.6 | async-start | bytes 6422528 | tf_op jit(solution)/shard_map/all_to_all | solution.py:233
  17.4 27.1 %collective-permute-start.8 = (bf16[256,896]{1,0:T(8,128)(2,1)S(1)}, bf16[256,896]{1,0:T(8,128)(2,1)S(1)}, u32[]{:S(2)}, u32[]{:S(2)}) collective-permute-start(bf16[256,896]{1,0:T(8,128)(2,1)S(1)} %get-tuple-element.208), channel_id=1, source_target_pairs={{0,3},{1,2},{2,1},{3,0},{4,7},{5,6},{6,5},{7,4},{8,11},{9,10},{10,... | collective-permute-start | bytes 1376264 | tf_op jit(solution)/shard_map/ppermute | solution.py:237
  21.1 39.7 %collective-permute-start.2 = (bf16[256,896]{1,0:T(8,128)(2,1)S(1)}, bf16[256,896]{1,0:T(8,128)(2,1)}, u32[]{:S(2)}, u32[]{:S(2)}) collective-permute-start(bf16[256,896]{1,0:T(8,128)(2,1)S(1)} %get-tuple-element.203), channel_id=1, source_target_pairs={{0,2},{1,3},{2,0},{3,1},{4,6},{5,7},{6,4},{7,5},{8,10},{9,11},{10,... | collective-permute-start | bytes 1376264 | tf_op jit(solution)/shard_map/ppermute | solution.py:237
  22.2 54.5 %collective-permute-start.3 = (bf16[256,896]{1,0:T(8,128)(2,1)S(1)}, bf16[256,896]{1,0:T(8,128)(2,1)}, u32[]{:S(2)}, u32[]{:S(2)}) collective-permute-start(bf16[256,896]{1,0:T(8,128)(2,1)S(1)} %get-tuple-element.204), channel_id=1, source_target_pairs={{0,3},{1,2},{2,1},{3,0},{4,7},{5,6},{6,5},{7,4},{8,11},{9,10},{10,... | collective-permute-start | bytes 1376264 | tf_op jit(solution)/shard_map/ppermute | solution.py:237
  22.9 67.4 %collective-permute-start.7 = (bf16[256,896]{1,0:T(8,128)(2,1)S(1)}, bf16[256,896]{1,0:T(8,128)(2,1)}, u32[]{:S(2)}, u32[]{:S(2)}) collective-permute-start(bf16[256,896]{1,0:T(8,128)(2,1)S(1)} %get-tuple-element.207), channel_id=1, source_target_pairs={{0,2},{1,3},{2,0},{3,1},{4,6},{5,7},{6,4},{7,5},{8,10},{9,11},{10,... | collective-permute-start | bytes 1376264 | tf_op jit(solution)/shard_map/ppermute | solution.py:237
  24.0 87.5 %collective-permute-start.1 = (bf16[512,896]{1,0:T(8,128)(2,1)S(1)}, bf16[512,896]{1,0:T(8,128)(2,1)}, u32[]{:S(2)}, u32[]{:S(2)}) collective-permute-start(bf16[512,896]{1,0:T(8,128)(2,1)S(1)} %get-tuple-element.202), channel_id=1, source_target_pairs={{0,1},{1,0},{2,3},{3,2},{4,5},{5,4},{6,7},{7,6},{8,9},{9,8},{10,11... | collective-permute-start | bytes 2752520 | tf_op jit(solution)/shard_map/ppermute | solution.py:237
  44.5 47.0 %collective-permute-start.10 = (bf16[256,896]{1,0:T(8,128)(2,1)S(1)}, bf16[256,896]{1,0:T(8,128)(2,1)S(1)}, u32[]{:S(2)}, u32[]{:S(2)}) collective-permute-start(bf16[256,896]{1,0:T(8,128)(2,1)S(1)} %collective-permute-done.8.refs_11_), channel_id=1, source_target_pairs={{0,16},{16,0},{1,17},{17,1},{2,18},{18,2},{3,19},{19,3},{4,20},{20... | collective-permute-start | bytes 1376264 | tf_op jit(solution)/shard_map/ppermute | solution.py:241
  60.7 50.9 %collective-permute-start.6 = (bf16[512,896]{1,0:T(8,128)(2,1)S(1)}, bf16[512,896]{1,0:T(8,128)(2,1)}, u32[]{:S(2)}, u32[]{:S(2)}) collective-permute-start(bf16[512,896]{1,0:T(8,128)(2,1)S(1)} %get-tuple-element.206), channel_id=1, source_target_pairs={{0,1},{1,0},{2,3},{3,2},{4,5},{5,4},{6,7},{7,6},{8,9},{9,8},{10,11... | collective-permute-start | bytes 2752520 | tf_op jit(solution)/shard_map/ppermute | solution.py:237
  76.8 16.0 %collective-permute-start.4 = (bf16[256,896]{1,0:T(8,128)(2,1)}, bf16[256,896]{1,0:T(8,128)(2,1)}, u32[]{:S(2)}, u32[]{:S(2)}) collective-permute-start(bf16[256,896]{1,0:T(8,128)(2,1)} %collective-permute-done.2.refs_2_), channel_id=1, source_target_pairs={{0,16},{16,0},{1,17},{17,1},{2,18},{18,2},{3,19},{19,3},{4,20},{20... | collective-permute-start | bytes 1376264 | tf_op jit(solution)/shard_map/ppermute | solution.py:241
  90.3 11.5 %collective-permute-start.5 = (bf16[256,896]{1,0:T(8,128)(2,1)}, bf16[256,896]{1,0:T(8,128)(2,1)}, u32[]{:S(2)}, u32[]{:S(2)}) collective-permute-start(bf16[256,896]{1,0:T(8,128)(2,1)} %collective-permute-done.3.refs_3_), channel_id=1, source_target_pairs={{0,16},{16,0},{1,17},{17,1},{2,18},{18,2},{3,19},{19,3},{4,20},{20... | collective-permute-start | bytes 1376264 | tf_op jit(solution)/shard_map/ppermute | solution.py:241
  91.5 0.8 copy-start.3
  92.3 19.2 %collective-permute-start.9 = (bf16[256,896]{1,0:T(8,128)(2,1)}, bf16[256,896]{1,0:T(8,128)(2,1)}, u32[]{:S(2)}, u32[]{:S(2)}) collective-permute-start(bf16[256,896]{1,0:T(8,128)(2,1)} %collective-permute-done.7.refs_10_), channel_id=1, source_target_pairs={{0,16},{16,0},{1,17},{17,1},{2,18},{18,2},{3,19},{19,3},{4,20},{20... | collective-permute-start | bytes 1376264 | tf_op jit(solution)/shard_map/ppermute | solution.py:241
  111.6 1.0 copy-start.4
  112.6 25.3 %copy-start.9 = (s32[32]{0:T(128)S(1)}, s32[32]{0:T(128)}, u32[]{:S(2)}) copy-start(s32[32]{0:T(128)} %param.11) | copy-start | bytes 388
  112.6 25.4 %copy-start.10 = (bf16[512,896]{1,0:T(8,128)(2,1)S(1)}, bf16[512,896]{1,0:T(8,128)(2,1)}, u32[]{:S(2)}) copy-start(bf16[512,896]{1,0:T(8,128)(2,1)} %get-tuple-element.201.refs_0_) | copy-start | bytes 2752516
  112.6 25.4 %copy-start.13 = (s32[32]{0:T(128)S(1)}, s32[32]{0:T(128)}, u32[]{:S(2)}) copy-start(s32[32]{0:T(128)} %param.10) | copy-start | bytes 388
  123.8 9.7 %collective-permute-start.11 = (bf16[4,224,128]{2,1,0:T(8,128)(2,1)S(1)}, bf16[4,224,128]{2,1,0:T(8,128)(2,1)S(1)}, u32[]{:S(2)}, u32[]{:S(2)}) collective-permute-start(bf16[4,224,128]{2,1,0:T(8,128)(2,1)S(1)} %shard_map.62), channel_id=1, source_target_pairs={{0,1},{1,0},{2,3},{3,2},{4,5},{5,4},{6,7},{7,6},{8,9},{9,8},{10,11... | collective-permute-start | bytes 688136 | tf_op jit(solution)/shard_map/ppermute | solution.py:237
  125.6 7.9 %collective-permute-start.12 = (bf16[4,224,128]{2,1,0:T(8,128)(2,1)S(1)}, bf16[4,224,128]{2,1,0:T(8,128)(2,1)S(1)}, u32[]{:S(2)}, u32[]{:S(2)}) collective-permute-start(bf16[4,224,128]{2,1,0:T(8,128)(2,1)S(1)} %shard_map.62), channel_id=1, source_target_pairs={{0,2},{1,3},{2,0},{3,1},{4,6},{5,7},{6,4},{7,5},{8,10},{9,11},{10,... | collective-permute-start | bytes 688136 | tf_op jit(solution)/shard_map/ppermute | solution.py:237
  126.8 11.1 %collective-permute-start.13 = (bf16[4,224,128]{2,1,0:T(8,128)(2,1)S(1)}, bf16[4,224,128]{2,1,0:T(8,128)(2,1)S(1)}, u32[]{:S(2)}, u32[]{:S(2)}) collective-permute-start(bf16[4,224,128]{2,1,0:T(8,128)(2,1)S(1)} %shard_map.62), channel_id=1, source_target_pairs={{0,3},{1,2},{2,1},{3,0},{4,7},{5,6},{6,5},{7,4},{8,11},{9,10},{10,... | collective-permute-start | bytes 688136 | tf_op jit(solution)/shard_map/ppermute | solution.py:237
  129.4 2.8 %collective-permute-start = (f32[1,1]{1,0:T(1,128)}, f32[1,1]{1,0:T(1,128)}, u32[]{:S(2)}, u32[]{:S(2)}) collective-permute-start(f32[1,1]{1,0:T(1,128)} %convert.4), channel_id=1, source_target_pairs={{0,16},{16,0},{1,17},{17,1},{2,18},{18,2},{3,19},{19,3},{4,20},{20... | collective-permute-start | bytes 20 | tf_op jit(solution)/shard_map/ppermute | solution.py:241
  138.2 0.7 copy-start.12
  150.2 1.7 copy-start
  151.8 77.8 %all-to-all-start.2 = ((bf16[16,112,896]{2,1,0:T(8,128)(2,1)}), bf16[16,112,896]{2,1,0:T(8,128)(2,1)S(1)}, u32[]{:S(2)}, u32[]{:S(2)}) async-start(bf16[16,112,896]{2,1,0:T(8,128)(2,1)} %copy-done), calls=%async_computation.2 | async-start | bytes 6422528 | tf_op jit(solution)/shard_map/cond/branch_2_fun/all_to_all | solution.py:233
  232.9 1.2 copy-start.8
where the time goes:
time: 235 us; the launch traced here: 234 us
  waiting for transfers between devices  156 us (66%)
  Pallas kernels  36 us (15%)
  starting transfers between devices  29.2 us (12%)
  local copies, waits for them, and re-layouts  5.82 us (2%)
  other arithmetic  4.6 us (2%)
    all_to_all x2, waiting for transfers between devices, exchange(): lax.all_to_all(value, 'adapter', split_axis=0, concat_axis=0, tiled=True)  71.2 us
    ppermute x9, waiting for transfers between devices, towards(): return lax.ppermute(value, 'adapter', [(i, i ^ k) for i in range(devices)])  65.1 us
    ppermute x5, waiting for transfers between devices, swapped(): return lax.ppermute(value, 'groups', [(0, 1), (1, 0)])  19.5 us
    all_to_all x2, starting transfers between devices, exchange(): lax.all_to_all(value, 'adapter', split_axis=0, concat_axis=0, tiled=True)  13.1 us
    pallas_call x1, Pallas kernels, back_and_mix(): call(up_kernel, jax.ShapeDtypeStruct((devices, kept, share), jnp.bfloat16...  11.3 us
    pallas_call x1, Pallas kernels, rows_to_quads(): call(down_kernel, jax.ShapeDtypeStruct((devices // 4, 2 * cap, LANES), bf...  11.1 us
    ppermute x9, starting transfers between devices, towards(): return lax.ppermute(value, 'adapter', [(i, i ^ k) for i in range(devices)])  10.1 us
    ppermute x5, starting transfers between devices, swapped(): return lax.ppermute(value, 'groups', [(0, 1), (1, 0)])  5.97 us
  transfers between devices with their start and end apart: 16, of which 9 were waited for; matrix products, arithmetic and copies ran while one was open for 1% of the time, Pallas kernels for 2%

commit v1 on v0

--- a/solution.py
+++ b/solution.py
@@ -81,10 +81,10 @@
     return lax.broadcasted_iota(jnp.int32, (rows, LANES), 1)
 
 
-def weight_kernel(whole, part_ref, group_ref, weight_ref, *out_refs):
+def weight_kernel(whole, which, part_ref, group_ref, weight_ref, *out_refs):
     quarter = LANES // QUAD
     inside = lanes_of(weight_ref.shape[0]) < quarter
-    for k, out_ref in enumerate(out_refs):
+    for k, out_ref in zip(which, out_refs):
         j = part_ref[k]
         count = out_ref.shape[0]
         start = 0 if k < 2 else pl.multiple_of(group_ref[0] * count, count)
@@ -303,23 +303,29 @@
         + [parts[2:] * resident + twin_half]
     ).astype(i32)
 
-    def dealt(weight):
-        counts = [columns, columns, columns // 2, columns // 2]
+    def shares(weight, which, after):
         values = call(
-            functools.partial(weight_kernel, whole),
-            [jax.ShapeDtypeStruct((count, share), bf16) for count in counts],
+            functools.partial(weight_kernel, whole, which),
+            [
+                jax.ShapeDtypeStruct((columns if k < 2 else columns // 2, share), bf16)
+                for k in which
+            ],
             [SMEM, SMEM, VMEM],
             0,
-            4 * columns * width,
+            len(which) * columns * width,
+            after,
         )(parts, group.reshape(1), weight)
-        near = [values[0], towards(values[1], 1, devices)]
-        return near, [towards(values[k], k, devices) for k in range(2, QUAD)]
-
-    down_near, down_far = dealt(adapter_down_weight.transpose(0, 2, 1).reshape(columns, width))
-    up_near, up_far = dealt(adapter_up_weight.reshape(columns, width))
-    down_weights = [*down_near, *down_far, *[swapped(value) for value in down_far]]
-    up_weights = [*up_near, *up_far, *[swapped(value) for value in up_far]]
-
+        return [towards(value, k, devices) if k else value for k, value in zip(which, values)]
+
+    weight = adapter_down_weight.transpose(0, 2, 1).reshape(columns, width)
+    down_weights = shares(weight, [0, 1, 2, 3], [])
+    down_weights.append(swapped(down_weights[2]))
+    weight = adapter_up_weight.reshape(columns, width)
+    up_weights = shares(weight, [0, 1, 2], down_weights[2:3])
+    up_weights += shares(weight, [3], down_weights[3:5])
+    down_weights.append(swapped(down_weights[3]))
+    up_weights.append(swapped(up_weights[2]))
+    up_weights.append(swapped(up_weights[3]))
     caps = [total * 5 // 16, total * 6 // 16, total * 7 // 16]
     cap = caps[-1]
     arrived = exchange(
@@ -334,14 +340,15 @@
     )
 
     most = jnp.max(arrived[:, 0, whole + LANES // QUAD + 1].astype(jnp.float32)).reshape(1, 1)
-    most = jnp.maximum(most, swapped(most))[0, 0].astype(i32)
+    others_most = swapped(most)
+    most = jnp.maximum(most, others_most)[0, 0].astype(i32)
     partial = call(
         down_kernel,
         jax.ShapeDtypeStruct((devices // 4, 2 * cap, LANES), bf16),
         [SMEM] + [VMEM] * (1 + len(down_weights)),
         2 * devices * cap * 4 * columns * share,
         2 * (devices * cap + 4 * columns) * share,
-        up_weights,
+        [up_weights[4], others_most],
     )(first, arrived, *down_weights)
     sums = [partial] + [towards(partial, k, devices) for k in range(1, QUAD)]
     return lax.switch(

time: 235 us -> 202 us (0.86)
  waiting for transfers between devices: 156 us -> 118 us
  starting transfers between devices: 29.2 us -> 36.4 us
    all_to_all x2, waiting for transfers between devices: 71.2 us -> 51.5 us  [exchange(): lax.all_to_all(value, 'adapter', split_axis=0, concat_axis=0, tiled=True)]
    ppermute x5, waiting for transfers between devices: 19.5 us -> 0.86 us  [swapped(): return lax.ppermute(value, 'groups', [(0, 1), (1, 0)])]
    ppermute x5, starting transfers between devices: 5.97 us -> 12.7 us  [swapped(): return lax.ppermute(value, 'groups', [(0, 1), (1, 0)])]
    pallas_call x2 -> x3, Pallas kernels: 5.28 us -> 7.09 us  [shares(): call(functools.partial(weight_kernel, whole, which), [jax.ShapeDtypeStruc...]
  transfers between devices with their start and end apart: 16 -> 16, of which waited for: 9 -> 8; matrix products, arithmetic and copies ran while one was open for 1% -> 1% of each run, Pallas kernels for 2% -> 9%
where the time goes in v1:
time: 202 us
  waiting for transfers between devices  118 us (58%)
  starting transfers between devices  36.4 us (18%)
  Pallas kernels  35.9 us (18%)
  other arithmetic  4.64 us (2%)
  local copies, waits for them, and re-layouts  4.26 us (2%)
  between operations  2.14 us (1%)
    ppermute x9, waiting for transfers between devices, towards(): return lax.ppermute(value, 'adapter', [(i, i ^ k) for i in range(devices)])  65.7 us
    all_to_all x2, waiting for transfers between devices, exchange(): lax.all_to_all(value, 'adapter', split_axis=0, concat_axis=0, tiled=True)  51.5 us
    all_to_all x2, starting transfers between devices, exchange(): lax.all_to_all(value, 'adapter', split_axis=0, concat_axis=0, tiled=True)  12.9 us
    ppermute x5, starting transfers between devices, swapped(): return lax.ppermute(value, 'groups', [(0, 1), (1, 0)])  12.7 us
    pallas_call x1, Pallas kernels, rows_to_quads(): call(down_kernel, jax.ShapeDtypeStruct((devices // 4, 2 * cap, LANES), bf...  11.5 us
    ppermute x9, starting transfers between devices, towards(): return lax.ppermute(value, 'adapter', [(i, i ^ k) for i in range(devices)])  10.7 us
    pallas_call x1, Pallas kernels, back_and_mix(): call(up_kernel, jax.ShapeDtypeStruct((devices, kept, share), jnp.bfloat16...  9.1 us
    pallas_call x3, Pallas kernels, shares(): call(functools.partial(weight_kernel, whole, which), [jax.ShapeDtypeStruc...  7.09 us
  transfers between devices with their start and end apart: 16, of which 8 were waited for; matrix products, arithmetic and copies ran while one was open for 1% of the time, Pallas kernels for 9%

profile of v1, /device:TPU:11, one launch (start us, length us, event | category | flops | bytes accessed | tf_op | source)
XLA Modules:
  0.0 201.7 jit_solution(1038547696524175899)
XLA Ops:
  3.1 5.5 %shard_map.59 = bf16[16,112,896]{2,1,0:T(8,128)(2,1)} custom-call(s32[1]{0:T(128)} %bitcast.14.most_ref, s32[1,256]{1,0:T(1,128)S(1)} %select_n.72.target_ref, f32[256,1]{1,0:T(8,128)S(1)} %convert_element_type.53.label_ref, bf16[256,3200]{1,0:T(8,128)(2,1)} %bitcast.30), custom_call_target="tpu_custom_call" | custom-call | flops 822083584 | bytes 4849664 | tf_op jit(solution)/shard_map/pallas_call | solution.py:332
  8.6 6.6 %all-to-all-start.6 = ((bf16[16,112,896]{2,1,0:T(8,128)(2,1)}), bf16[16,112,896]{2,1,0:T(8,128)(2,1)}, u32[]{:S(2)}, u32[]{:S(2)}) async-start(bf16[16,112,896]{2,1,0:T(8,128)(2,1)} %shard_map.59), calls=%async_computation.6 | async-start | bytes 6422528 | tf_op jit(solution)/shard_map/all_to_all | solution.py:233
  15.2 3.2 %shard_map.60 = (bf16[512,896]{1,0:T(8,128)(2,1)S(1)}, bf16[512,896]{1,0:T(8,128)(2,1)}, bf16[256,896]{1,0:T(8,128)(2,1)S(1)}, bf16[256,896]{1,0:T(8,128)(2,1)S(1)}) custom-call(s32[4]{0:T(128)S(1)} %iota_xor_fusion.part_ref.refs_1_.refs_2_, s32[1]{0:T(128)} %bitcast.20.group_ref.refs_2_.refs_3_, bf16[512,3200]{1,0:T(8,128)(2,1)} %bitcast.38), custom_call_target="tpu_custom_call" | custom-call | bytes 6553600 | tf_op jit(solution)/shard_map/pallas_call | solution.py:307
  18.7 1.7 collective-permute-start.5
  20.4 23.1 %collective-permute-done.1.refs_0_.refs_6_ = bf16[256,896]{1,0:T(8,128)(2,1)S(1)} collective-permute-done((bf16[256,896]{1,0:T(8,128)(2,1)S(1)}, bf16[256,896]{1,0:T(8,128)(2,1)S(1)}, u32[]{:S(2)}, u32[]{:S(2)}) %collective-permute-start.1) | collective-permute-done | bytes 458784 | tf_op jit(solution)/shard_map/ppermute | solution.py:237
  44.8 3.2 %shard_map.61 = (bf16[512,896]{1,0:T(8,128)(2,1)}, bf16[512,896]{1,0:T(8,128)(2,1)S(1)}, bf16[256,896]{1,0:T(8,128)(2,1)}) custom-call(bf16[256,896]{1,0:T(8,128)(2,1)S(1)} %collective-permute-done.1.refs_0_.refs_6_, s32[4]{0:T(128)S(1)} %iota_xor_fusion.part_ref.refs_1_.refs_2_, s32[1]{0:T(128)} %bitcast.20.group_ref.refs_2_.refs_3_, bf16[512,3200]{1,0:T(8,128)(2,1)} %bitcast.35), custom_call_target="tpu_custom_call" | custom-call | bytes 4915200 | tf_op jit(solution)/shard_map/pallas_call | solution.py:307
  48.0 2.2 %collective-permute-start.2 = (bf16[256,896]{1,0:T(8,128)(2,1)}, bf16[256,896]{1,0:T(8,128)(2,1)}, u32[]{:S(2)}, u32[]{:S(2)}) collective-permute-start(bf16[256,896]{1,0:T(8,128)(2,1)} %get-tuple-element.201), channel_id=1, source_target_pairs={{0,2},{1,3},{2,0},{3,1},{4,6},{5,7},{6,4},{7,5},{8,10},{9,11},{10,... | collective-permute-start | bytes 1376264 | tf_op jit(solution)/shard_map/ppermute | solution.py:237
  50.3 1.8 collective-permute-start.4
  52.1 10.9 %collective-permute-done.5.refs_7_.refs_0_ = bf16[256,896]{1,0:T(8,128)(2,1)S(1)} collective-permute-done((bf16[256,896]{1,0:T(8,128)(2,1)S(1)}, bf16[256,896]{1,0:T(8,128)(2,1)S(1)}, u32[]{:S(2)}, u32[]{:S(2)}) %collective-permute-start.5) | collective-permute-done | bytes 458784 | tf_op jit(solution)/shard_map/ppermute | solution.py:237
  65.3 10.8 %collective-permute-done.2 = bf16[256,896]{1,0:T(8,128)(2,1)} collective-permute-done((bf16[256,896]{1,0:T(8,128)(2,1)}, bf16[256,896]{1,0:T(8,128)(2,1)}, u32[]{:S(2)}, u32[]{:S(2)}) %collective-permute-start.2) | collective-permute-done | bytes 458784 | tf_op jit(solution)/shard_map/ppermute | solution.py:237
  77.6 1.6 collective-permute-start.11
  79.2 11.2 %collective-permute-done.12 = bf16[256,896]{1,0:T(8,128)(2,1)} collective-permute-done((bf16[256,896]{1,0:T(8,128)(2,1)S(1)}, bf16[256,896]{1,0:T(8,128)(2,1)}, u32[]{:S(2)}, u32[]{:S(2)}) %collective-permute-start.12) | collective-permute-done | bytes 458784 | tf_op jit(solution)/shard_map/ppermute | solution.py:237
  91.7 1.5 slice_reduce_fusion
  93.9 7.8 %collective-permute-start = (f32[1,1]{1,0:T(1,128)}, f32[1,1]{1,0:T(1,128)}, u32[]{:S(2)}, u32[]{:S(2)}) collective-permute-start(f32[1,1]{1,0:T(1,128)} %convert.4), channel_id=1, source_target_pairs={{0,16},{16,0},{1,17},{17,1},{2,18},{18,2},{3,19},{19,3},{4,20},{20... | collective-permute-start | bytes 20 | tf_op jit(solution)/shard_map/ppermute | solution.py:241
  103.7 11.5 %shard_map.62 = bf16[4,224,128]{2,1,0:T(8,128)(2,1)S(1)} custom-call(bf16[256,896]{1,0:T(8,128)(2,1)} %collective-permute-done.3.refs_0_, f32[1,1]{1,0:T(1,128)} %collective-permute-done.refs_1_, s32[6]{0:T(128)S(1)} %pad_add_fusion.refs_2_, bf16[16,112,896]{2,1,0:T(8,128)(2,1)} %all-to-all-done.6.refs_3_, bf16[512,896]{1,0:T(8,128)(2,1)S(1)} %copy-done.4, ...), custom_call_target="tpu_custom_call" | custom-call | flops 6576668672 | bytes 6881280 | tf_op jit(solution)/shard_map/pallas_call | solution.py:345
  115.2 2.3 %collective-permute-start.10 = (bf16[4,224,128]{2,1,0:T(8,128)(2,1)S(1)}, bf16[4,224,128]{2,1,0:T(8,128)(2,1)S(1)}, u32[]{:S(2)}, u32[]{:S(2)}) collective-permute-start(bf16[4,224,128]{2,1,0:T(8,128)(2,1)S(1)} %shard_map.62), channel_id=1, source_target_pairs={{0,3},{1,2},{2,1},{3,0},{4,7},{5,6},{6,5},{7,4},{8,11},{9,10},{10,... | collective-permute-start | bytes 688136 | tf_op jit(solution)/shard_map/ppermute | solution.py:237
  119.2 4.8 %collective-permute-done.10 = bf16[4,224,128]{2,1,0:T(8,128)(2,1)S(1)} collective-permute-done((bf16[4,224,128]{2,1,0:T(8,128)(2,1)S(1)}, bf16[4,224,128]{2,1,0:T(8,128)(2,1)S(1)}, u32[]{:S(2)}, u32[]{:S(2)}) %collective-permute-start.10) | collective-permute-done | bytes 229408 | tf_op jit(solution)/shard_map/ppermute | solution.py:237
  124.0 4.9 %collective-permute-done.9 = bf16[4,224,128]{2,1,0:T(8,128)(2,1)S(1)} collective-permute-done((bf16[4,224,128]{2,1,0:T(8,128)(2,1)S(1)}, bf16[4,224,128]{2,1,0:T(8,128)(2,1)S(1)}, u32[]{:S(2)}, u32[]{:S(2)}) %collective-permute-start.9) | collective-permute-done | bytes 229408 | tf_op jit(solution)/shard_map/ppermute | solution.py:237
  129.0 71.5 %conditional.1 = (bf16[32,8,3200]{2,1,0:T(8,128)(2,1)S(1)}) conditional(s32[]{:T(128)} %bitcast.18, (s32[32,8]{1,0:T(8,128)S(1)}, s32[32,8]{1,0:T(8,128)S(1)}, s32[32,8]{1,0:T(8,128)S(1)}, s32[32,8]{1,0:T(8,128)S(1)}, bf16[32,8,3200]{2,1,0:T(8,128)(2,1)}, /*index=5*/s32[6]{0:T(128)S(1)}, ...), branch_computations={%region_4.5_spmd, %region_5.6_spmd, %region_6.7_spmd, %region_7.12... | conditional | flops 7398753280 | bytes 120688824 | solution.py:354
  129.0 9.1 %branch_0_fun.2 = bf16[16,80,896]{2,1,0:T(8,128)(2,1)S(1)} custom-call(s32[6]{0:T(128)S(1)} %get-tuple-element.142.first_ref, bf16[16,112,896]{2,1,0:T(8,128)(2,1)} %get-tuple-element.143.rows_ref, bf16[4,224,128]{2,1,0:T(8,128)(2,1)S(1)} %get-tuple-element.144.refs_0_, bf16[4,224,128]{2,1,0:T(8,128)(2,1)S(1)} %get-tuple-element.145.refs_1_, ...), custom_call_target="tpu_custom_call" | custom-call | flops 4697620480 | bytes 8257536 | tf_op jit(solution)/shard_map/cond/branch_0_fun/pallas_call | solution.py:251
  138.2 1.4 copy-done.2
  139.6 6.4 %all-to-all-start = ((bf16[16,80,896]{2,1,0:T(8,128)(2,1)}), bf16[16,80,896]{2,1,0:T(8,128)(2,1)S(1)}, u32[]{:S(2)}, u32[]{:S(2)}) async-start(bf16[16,80,896]{2,1,0:T(8,128)(2,1)} %copy-done.2), calls=%async_computation | async-start | bytes 4587520 | tf_op jit(solution)/shard_map/cond/branch_0_fun/all_to_all | solution.py:233
  146.0 51.5 %all-to-all-done.returned_ref = bf16[16,80,896]{2,1,0:T(8,128)(2,1)S(1)} async-done(((bf16[16,80,896]{2,1,0:T(8,128)(2,1)}), bf16[16,80,896]{2,1,0:T(8,128)(2,1)S(1)}, u32[]{:S(2)}, u32[]{:S(2)}) %all-to-all-start) | async-done | bytes 2293792 | tf_op jit(solution)/shard_map/cond/branch_0_fun/all_to_all | solution.py:233
  197.6 2.7 %branch_0_fun.3 = bf16[256,3200]{1,0:T(8,128)(2,1)S(1)} custom-call(s32[256,1]{1,0:T(8,128)S(1)} %reshape_reshape.10.target_ref, bf16[256,3200]{1,0:T(8,128)(2,1)} %bitcast.31, bf16[16,80,896]{2,1,0:T(8,128)(2,1)S(1)} %all-to-all-done.returned_ref), custom_call_target="tpu_custom_call" | custom-call | flops 587202560 | bytes 5570560 | tf_op jit(solution)/shard_map/cond/branch_0_fun/pallas_call | solution.py:258
  (49 shorter events, 13.5 us)
Async XLA Ops:
  8.6 83.1 %all-to-all-start.6 = ((bf16[16,112,896]{2,1,0:T(8,128)(2,1)}), bf16[16,112,896]{2,1,0:T(8,128)(2,1)}, u32[]{:S(2)}, u32[]{:S(2)}) async-start(bf16[16,112,896]{2,1,0:T(8,128)(2,1)} %shard_map.59), calls=%async_computation.6 | async-start | bytes 6422528 | tf_op jit(solution)/shard_map/all_to_all | solution.py:233
  15.2 47.8 %copy-start.6 = (bf16[8,64,3200]{2,1,0:T(8,128)(2,1)S(1)}, bf16[8,64,3200]{2,1,0:T(8,128)(2,1)}, u32[]{:S(2)}) copy-start(bf16[8,64,3200]{2,1,0:T(8,128)(2,1)} %param.13) | copy-start | bytes 9830404
  18.4 45.2 %copy-start.3 = (bf16[512,896]{1,0:T(8,128)(2,1)}, bf16[512,896]{1,0:T(8,128)(2,1)S(1)}, u32[]{:S(2)}) copy-start(bf16[512,896]{1,0:T(8,128)(2,1)S(1)} %get-tuple-element.202.refs_4_) | copy-start | bytes 2752516
  18.4 25.1 %collective-permute-start.1 = (bf16[256,896]{1,0:T(8,128)(2,1)S(1)}, bf16[256,896]{1,0:T(8,128)(2,1)S(1)}, u32[]{:S(2)}, u32[]{:S(2)}) collective-permute-start(bf16[256,896]{1,0:T(8,128)(2,1)S(1)} %get-tuple-element.200), channel_id=1, source_target_pairs={{0,2},{1,3},{2,0},{3,1},{4,6},{5,7},{6,4},{7,5},{8,10},{9,11},{10,... | collective-permute-start | bytes 1376264 | tf_op jit(solution)/shard_map/ppermute | solution.py:237
  18.7 44.2 %collective-permute-start.5 = (bf16[256,896]{1,0:T(8,128)(2,1)S(1)}, bf16[256,896]{1,0:T(8,128)(2,1)S(1)}, u32[]{:S(2)}, u32[]{:S(2)}) collective-permute-start(bf16[256,896]{1,0:T(8,128)(2,1)S(1)} %get-tuple-element.204), channel_id=1, source_target_pairs={{0,3},{1,2},{2,1},{3,0},{4,7},{5,6},{6,5},{7,4},{8,11},{9,10},{10,... | collective-permute-start | bytes 1376264 | tf_op jit(solution)/shard_map/ppermute | solution.py:237
  43.6 19.4 %collective-permute-start.6 = (bf16[256,896]{1,0:T(8,128)(2,1)S(1)}, bf16[256,896]{1,0:T(8,128)(2,1)S(1)}, u32[]{:S(2)}, u32[]{:S(2)}) collective-permute-start(bf16[256,896]{1,0:T(8,128)(2,1)S(1)} %collective-permute-done.1.refs_0_.refs_6_), channel_id=1, source_target_pairs={{0,16},{16,0},{1,17},{17,1},{2,18},{18,2},{3,19},{19,3},{4,20},{20... | collective-permute-start | bytes 1376264 | tf_op jit(solution)/shard_map/ppermute | solution.py:241
  48.0 28.1 %collective-permute-start.2 = (bf16[256,896]{1,0:T(8,128)(2,1)}, bf16[256,896]{1,0:T(8,128)(2,1)}, u32[]{:S(2)}, u32[]{:S(2)}) collective-permute-start(bf16[256,896]{1,0:T(8,128)(2,1)} %get-tuple-element.201), channel_id=1, source_target_pairs={{0,2},{1,3},{2,0},{3,1},{4,6},{5,7},{6,4},{7,5},{8,10},{9,11},{10,... | collective-permute-start | bytes 1376264 | tf_op jit(solution)/shard_map/ppermute | solution.py:237
  50.3 51.5 %collective-permute-start.4 = (bf16[512,896]{1,0:T(8,128)(2,1)}, bf16[512,896]{1,0:T(8,128)(2,1)}, u32[]{:S(2)}, u32[]{:S(2)}) collective-permute-start(bf16[512,896]{1,0:T(8,128)(2,1)} %get-tuple-element.203), channel_id=1, source_target_pairs={{0,1},{1,0},{2,3},{3,2},{4,5},{5,4},{6,7},{7,6},{8,9},{9,8},{10,11... | collective-permute-start | bytes 2752520 | tf_op jit(solution)/shard_map/ppermute | solution.py:237
  63.6 26.8 %collective-permute-start.12 = (bf16[256,896]{1,0:T(8,128)(2,1)S(1)}, bf16[256,896]{1,0:T(8,128)(2,1)}, u32[]{:S(2)}, u32[]{:S(2)}) collective-permute-start(bf16[256,896]{1,0:T(8,128)(2,1)S(1)} %shard_map.63), channel_id=1, source_target_pairs={{0,3},{1,2},{2,1},{3,0},{4,7},{5,6},{6,5},{7,4},{8,11},{9,10},{10,... | collective-permute-start | bytes 1376264 | tf_op jit(solution)/shard_map/ppermute | solution.py:237
  64.1 29.8 %collective-permute-start.7 = (bf16[256,896]{1,0:T(8,128)(2,1)S(1)}, bf16[256,896]{1,0:T(8,128)(2,1)S(1)}, u32[]{:S(2)}, u32[]{:S(2)}) collective-permute-start(bf16[256,896]{1,0:T(8,128)(2,1)S(1)} %collective-permute-done.5.refs_7_.refs_0_), channel_id=1, source_target_pairs={{0,16},{16,0},{1,17},{17,1},{2,18},{18,2},{3,19},{19,3},{4,20},{20... | collective-permute-start | bytes 1376264 | tf_op jit(solution)/shard_map/ppermute | solution.py:241
  76.1 25.6 %collective-permute-start.3 = (bf16[256,896]{1,0:T(8,128)(2,1)}, bf16[256,896]{1,0:T(8,128)(2,1)}, u32[]{:S(2)}, u32[]{:S(2)}) collective-permute-start(bf16[256,896]{1,0:T(8,128)(2,1)} %collective-permute-done.2), channel_id=1, source_target_pairs={{0,16},{16,0},{1,17},{17,1},{2,18},{18,2},{3,19},{19,3},{4,20},{20... | collective-permute-start | bytes 1376264 | tf_op jit(solution)/shard_map/ppermute | solution.py:241
  77.6 41.6 %collective-permute-start.11 = (bf16[512,896]{1,0:T(8,128)(2,1)S(1)}, bf16[512,896]{1,0:T(8,128)(2,1)}, u32[]{:S(2)}, u32[]{:S(2)}) collective-permute-start(bf16[512,896]{1,0:T(8,128)(2,1)S(1)} %get-tuple-element.206), channel_id=1, source_target_pairs={{0,1},{1,0},{2,3},{3,2},{4,5},{5,4},{6,7},{7,6},{8,9},{9,8},{10,11... | collective-permute-start | bytes 2752520 | tf_op jit(solution)/shard_map/ppermute | solution.py:237
  90.4 28.8 %collective-permute-start.13 = (bf16[256,896]{1,0:T(8,128)(2,1)}, bf16[256,896]{1,0:T(8,128)(2,1)S(1)}, u32[]{:S(2)}, u32[]{:S(2)}) collective-permute-start(bf16[256,896]{1,0:T(8,128)(2,1)} %collective-permute-done.12), channel_id=1, source_target_pairs={{0,16},{16,0},{1,17},{17,1},{2,18},{18,2},{3,19},{19,3},{4,20},{20... | collective-permute-start | bytes 1376264 | tf_op jit(solution)/shard_map/ppermute | solution.py:241
  93.9 8.6 %collective-permute-start = (f32[1,1]{1,0:T(1,128)}, f32[1,1]{1,0:T(1,128)}, u32[]{:S(2)}, u32[]{:S(2)}) collective-permute-start(f32[1,1]{1,0:T(1,128)} %convert.4), channel_id=1, source_target_pairs={{0,16},{16,0},{1,17},{17,1},{2,18},{18,2},{3,19},{19,3},{4,20},{20... | collective-permute-start | bytes 20 | tf_op jit(solution)/shard_map/ppermute | solution.py:241
  102.6 1.2 copy-start.4
  103.7 25.2 %copy-start.10 = (s32[32]{0:T(128)S(1)}, s32[32]{0:T(128)}, u32[]{:S(2)}) copy-start(s32[32]{0:T(128)} %param.11) | copy-start | bytes 388
  103.7 25.3 %copy-start.13 = (s32[32]{0:T(128)S(1)}, s32[32]{0:T(128)}, u32[]{:S(2)}) copy-start(s32[32]{0:T(128)} %param.10) | copy-start | bytes 388
  115.2 8.7 %collective-permute-start.10 = (bf16[4,224,128]{2,1,0:T(8,128)(2,1)S(1)}, bf16[4,224,128]{2,1,0:T(8,128)(2,1)S(1)}, u32[]{:S(2)}, u32[]{:S(2)}) collective-permute-start(bf16[4,224,128]{2,1,0:T(8,128)(2,1)S(1)} %shard_map.62), channel_id=1, source_target_pairs={{0,3},{1,2},{2,1},{3,0},{4,7},{5,6},{6,5},{7,4},{8,11},{9,10},{10,... | collective-permute-start | bytes 688136 | tf_op jit(solution)/shard_map/ppermute | solution.py:237
  117.6 6.4 %collective-permute-start.8 = (bf16[4,224,128]{2,1,0:T(8,128)(2,1)S(1)}, bf16[4,224,128]{2,1,0:T(8,128)(2,1)S(1)}, u32[]{:S(2)}, u32[]{:S(2)}) collective-permute-start(bf16[4,224,128]{2,1,0:T(8,128)(2,1)S(1)} %shard_map.62), channel_id=1, source_target_pairs={{0,1},{1,0},{2,3},{3,2},{4,5},{5,4},{6,7},{7,6},{8,9},{9,8},{10,11... | collective-permute-start | bytes 688136 | tf_op jit(solution)/shard_map/ppermute | solution.py:237
  117.6 11.3 %collective-permute-start.9 = (bf16[4,224,128]{2,1,0:T(8,128)(2,1)S(1)}, bf16[4,224,128]{2,1,0:T(8,128)(2,1)S(1)}, u32[]{:S(2)}, u32[]{:S(2)}) collective-permute-start(bf16[4,224,128]{2,1,0:T(8,128)(2,1)S(1)} %shard_map.62), channel_id=1, source_target_pairs={{0,2},{1,3},{2,0},{3,1},{4,6},{5,7},{6,4},{7,5},{8,10},{9,11},{10,... | collective-permute-start | bytes 688136 | tf_op jit(solution)/shard_map/ppermute | solution.py:237
  138.1 1.4 copy-start.2
  139.6 58.0 %all-to-all-start = ((bf16[16,80,896]{2,1,0:T(8,128)(2,1)}), bf16[16,80,896]{2,1,0:T(8,128)(2,1)S(1)}, u32[]{:S(2)}, u32[]{:S(2)}) async-start(bf16[16,80,896]{2,1,0:T(8,128)(2,1)} %copy-done.2), calls=%async_computation | async-start | bytes 4587520 | tf_op jit(solution)/shard_map/cond/branch_0_fun/all_to_all | solution.py:233
  200.6 1.2 copy-start.9

commit v2 on v1

--- a/solution.py
+++ b/solution.py
@@ -10,6 +10,9 @@
 LANES = 128
 HALF = 64
 QUAD = 4
+QUARTER = 32
+STEP = 16
+NOTE = 96
 VMEM = pl.BlockSpec(memory_space=pltpu.VMEM)
 SMEM = pl.BlockSpec(memory_space=pltpu.SMEM)
 
@@ -82,132 +85,248 @@
 
 
 def weight_kernel(whole, which, part_ref, group_ref, weight_ref, *out_refs):
-    quarter = LANES // QUAD
-    inside = lanes_of(weight_ref.shape[0]) < quarter
+    tiles = whole // LANES
     for k, out_ref in zip(which, out_refs):
         j = part_ref[k]
-        count = out_ref.shape[0]
-        start = 0 if k < 2 else pl.multiple_of(group_ref[0] * count, count)
-        rows = pl.ds(start, count)
-        out_ref[:, 0:whole] = weight_ref[rows, pl.ds(pl.multiple_of(j * whole, LANES), whole)]
-        last = weight_ref[rows, QUAD * whole :].astype(jnp.float32)
-        turned = pltpu.roll(last, lax.rem(LANES - quarter * j, LANES), 1)
-        out_ref[:, whole:] = jnp.where(inside[0:count], turned, 0.0).astype(jnp.bfloat16)
-
-
-def pack_kernel(whole, most_ref, target_ref, label_ref, tokens_ref, out_ref, normed_ref):
+        if k < 2:
+            last = weight_ref[:, QUAD * whole :].astype(jnp.float32)
+            turned = pltpu.roll(last, lax.rem(LANES - QUARTER * j, LANES), 1)
+            inside = lanes_of(last.shape[0]) < QUARTER
+            out_ref[:, 0:whole] = weight_ref[:, pl.ds(pl.multiple_of(j * whole, LANES), whole)]
+            out_ref[:, whole:] = jnp.where(inside, turned, 0.0).astype(jnp.bfloat16)
+            continue
+        count = weight_ref.shape[0] // 2
+        start = pl.multiple_of(group_ref[0] * count, count)
+        for t in range(tiles):
+            column = pl.multiple_of(j * whole + t * LANES, LANES)
+            out_ref[t * count : (t + 1) * count, :] = weight_ref[
+                pl.ds(start, count), pl.ds(column, LANES)
+            ]
+        last = weight_ref[pl.ds(start, count), QUAD * whole :].astype(jnp.float32)
+        size = count // QUAD
+        owner = lanes_of(size) // QUARTER
+        merged = jnp.zeros((size, LANES), jnp.float32)
+        for m in range(QUAD):
+            shift = lax.rem(LANES + QUARTER * (m - j), LANES)
+            turned = pltpu.roll(last[m * size : (m + 1) * size], shift, 1)
+            merged = jnp.where(owner == m, turned, merged)
+        out_ref[tiles * count :, :] = merged.astype(jnp.bfloat16)
+
+
+def open_far(far_refs, opened_ref):
+    count, width = opened_ref.shape[1:]
+    tiles, size = width // LANES - 1, count // QUAD
+    inside = lanes_of(size) < QUARTER
+    for i, ref in enumerate(far_refs):
+        for t in range(tiles):
+            opened_ref[i, :, t * LANES : (t + 1) * LANES] = ref[t * count : (t + 1) * count, :]
+        packed = ref[tiles * count :, :].astype(jnp.float32)
+        for m in range(QUAD):
+            turned = pltpu.roll(packed, (LANES - QUARTER * m) % LANES, 1) if m else packed
+            opened_ref[i, m * size : (m + 1) * size, tiles * LANES :] = jnp.where(
+                inside, turned, 0.0
+            ).astype(jnp.bfloat16)
+
+
+def pack_kernel(whole, cap, most_ref, target_ref, label_ref, tokens_ref, out_ref, normed_ref):
     values = tokens_ref[...].astype(jnp.float32)
     mean_sq = jnp.mean(values * values, axis=-1, keepdims=True)
     normed_ref[...] = (values * lax.rsqrt(mean_sq + 1e-06)).astype(jnp.bfloat16)
     total = tokens_ref.shape[0]
-    quads, cap = out_ref.shape[0] // QUAD, out_ref.shape[1]
-    quarter = LANES // QUAD
+    quads, tiles = out_ref.shape[0] // QUAD, whole // LANES
     lane = lanes_of(total)
     last = normed_ref[:, QUAD * whole :].astype(jnp.float32)
-    label = jnp.where(lane == quarter, label_ref[...], 0.0)
+    label = jnp.where(lane == QUARTER, label_ref[...], 0.0)
     ends = []
     for j in range(QUAD):
-        turned = pltpu.roll(last, (LANES - quarter * j) % LANES, 1) if j else last
-        ends.append(jnp.where(lane < quarter, turned, label).astype(jnp.bfloat16))
+        turned = pltpu.roll(last, (LANES - QUARTER * j) % LANES, 1) if j else last
+        ends.append(jnp.where(lane < QUARTER, turned, label).astype(jnp.bfloat16))
     most = most_ref[0].astype(jnp.float32)
-    note = jnp.where(lanes_of(cap) == quarter + 1, most, 0.0)
+    group_lane = lanes_of(QUARTER) // QUARTER
+    step_lane = lanes_of(STEP)
     for q in range(quads):
         place = lax.broadcasted_iota(jnp.int32, (cap, total), 0) + q * total
         chosen = jnp.where(target_ref[...] == place, 1.0, 0.0).astype(jnp.bfloat16)
         for j in range(QUAD):
-            columns = slice(j * whole, (j + 1) * whole)
-            out_ref[q * QUAD + j, :, 0:whole] = jnp.dot(
-                chosen, normed_ref[:, columns], preferred_element_type=jnp.float32
+            share = jnp.dot(
+                chosen,
+                normed_ref[:, j * whole : (j + 1) * whole],
+                preferred_element_type=jnp.float32,
             ).astype(jnp.bfloat16)
+            for t in range(tiles):
+                out_ref[q * QUAD + j, t * cap : (t + 1) * cap, :] = share[
+                    :, t * LANES : (t + 1) * LANES
+                ]
             end = jnp.dot(chosen, ends[j], preferred_element_type=jnp.float32)
-            out_ref[q * QUAD + j, :, whole:] = (end + note).astype(jnp.bfloat16)
-
-
-def label_of(last_tile):
-    rows = last_tile.shape[0]
-    quarter = LANES // QUAD
-    label = last_tile[:, quarter : quarter + 1].astype(jnp.float32) - 1.0
-    return label - jnp.where(lanes_of(rows) < HALF, 0.0, 1.0)
+            if j == 0:
+                notes = jnp.where(step_lane == NOTE + cap // STEP, most, 0.0)
+                for a in range(cap // STEP):
+                    turned = pltpu.roll(end[a * STEP : (a + 1) * STEP], NOTE + a - QUARTER, 1)
+                    notes = jnp.where(step_lane == NOTE + a, turned, notes)
+            padded = jnp.concatenate(
+                [end, jnp.zeros((QUAD * QUARTER - cap, LANES), jnp.float32)], axis=0
+            )
+            merged = padded[0:QUARTER]
+            for m in range(1, QUAD):
+                turned = pltpu.roll(padded[m * QUARTER : (m + 1) * QUARTER], m * QUARTER, 1)
+                merged = jnp.where(group_lane == m, turned, merged)
+            out_ref[q * QUAD + j, tiles * cap : tiles * cap + STEP, :] = merged[0:STEP].astype(
+                jnp.bfloat16
+            )
+            out_ref[q * QUAD + j, tiles * cap + STEP :, :] = jnp.where(
+                step_lane >= NOTE, notes, merged[STEP:]
+            ).astype(jnp.bfloat16)
+
+
+def step_labels(cap, tiles, a, rows_ref):
+    columns = []
+    for s in range(rows_ref.shape[0]):
+        notes = rows_ref[s, tiles * cap + STEP :, :].astype(jnp.float32)
+        turned = pltpu.roll(notes, lax.rem(2 * LANES - NOTE - a, LANES), 1)
+        columns.append(jnp.broadcast_to(turned[:, 0:1], (STEP, LANES)))
+    label = jnp.concatenate(columns, axis=0) - 1.0
+    return label, label - jnp.where(lanes_of(label.shape[0]) < HALF, 0.0, 1.0)
+
+
+def weight_blocks(near_refs, opened_ref):
+    return [ref[...] for ref in near_refs] + [opened_ref[i] for i in range(opened_ref.shape[0])]
 
 
 def down_kernel(first_ref, rows_ref, *refs):
-    weight_refs, out_ref = refs[:-1], refs[-1]
-    senders, cap, width = rows_ref.shape
+    near_refs, far_refs, (out_ref, opened_ref, batch_ref) = refs[:2], refs[2:6], refs[6:]
+    senders, width = rows_ref.shape[0], batch_ref.shape[1]
+    tiles = width // LANES - 1
+    cap = out_ref.shape[0] * STEP
     dims = (((1,), (1,)), ((), ()))
-    low = lanes_of(2 * cap) < HALF
-
-    def one(c, carry):
-        rows = jnp.concatenate([rows_ref[4 * c + i] for i in range(4)], axis=0)
-        label = label_of(rows[:, width - LANES :])
-        picked = jnp.zeros((4 * cap, LANES), jnp.float32)
-        for k, weight_ref in enumerate(weight_refs):
-            product = lax.dot_general(
-                rows, weight_ref[...], dims, preferred_element_type=jnp.float32
+    half = senders * STEP // 2
+    low = lanes_of(half) < HALF
+    open_far(far_refs, opened_ref)
+
+    def one(a, carry):
+        label, lowered = step_labels(cap, tiles, a, rows_ref)
+        used = jnp.max(label) >= 0.0
+        out_ref[a] = jnp.zeros((half, LANES), jnp.bfloat16)
+
+        @pl.when(used)
+        def _():
+            shift = lax.rem(LANES - QUARTER * (a // 2), LANES)
+            spot = pl.multiple_of(tiles * cap + lax.rem(a, 2) * STEP, STEP)
+            for s in range(senders):
+                rows = slice(s * STEP, (s + 1) * STEP)
+                for t in range(tiles):
+                    at = pl.multiple_of(t * cap + a * STEP, STEP)
+                    batch_ref[rows, t * LANES : (t + 1) * LANES] = rows_ref[s, pl.ds(at, STEP), :]
+                end = rows_ref[s, pl.ds(spot, STEP), :].astype(jnp.float32)
+                batch_ref[rows, tiles * LANES :] = pltpu.roll(end, shift, 1).astype(jnp.bfloat16)
+            picked = jnp.zeros((senders * STEP, LANES), jnp.float32)
+            for k, weight in enumerate(weight_blocks(near_refs, opened_ref)):
+                product = lax.dot_general(
+                    batch_ref[...], weight, dims, preferred_element_type=jnp.float32
+                )
+                first = first_ref[k].astype(jnp.float32)
+                for t in range(weight.shape[0] // LANES):
+                    columns = slice(t * LANES, (t + 1) * LANES)
+                    picked = jnp.where(lowered == first + 2.0 * t, product[:, columns], picked)
+            both = picked + pltpu.roll(picked, HALF, 1)
+            out_ref[a] = jnp.where(low, both[0:half], both[half:]).astype(jnp.bfloat16)
+
+        return carry
+
+    lax.fori_loop(0, cap // STEP, one, 0)
+
+
+def up_kernel(first_ref, rows_ref, *refs):
+    sum_refs, near_refs, far_refs = refs[:QUAD], refs[QUAD : QUAD + 2], refs[QUAD + 2 : QUAD + 6]
+    out_ref, opened_ref, ends_ref = refs[QUAD + 6 :]
+    senders, width = rows_ref.shape[0], opened_ref.shape[2]
+    tiles = width // LANES - 1
+    cap = sum_refs[0].shape[0] * STEP
+    kept = (out_ref.shape[1] - QUARTER) // tiles
+    half = senders * STEP // 2
+    low = lanes_of(half) < HALF
+    group_lane = lanes_of(STEP) // QUARTER
+    open_far(far_refs, opened_ref)
+    ends_ref[...] = jnp.zeros(ends_ref.shape, jnp.float32)
+
+    def one(a, carry):
+        label, lowered = step_labels(cap, tiles, a, rows_ref)
+        used = jnp.max(label) >= 0.0
+
+        def leave(value):
+            spot = pl.multiple_of(lax.rem(a, 2) * STEP, STEP)
+            for s in range(senders):
+                rows = slice(s * STEP, (s + 1) * STEP)
+                for t in range(tiles):
+                    at = pl.multiple_of(t * kept + a * STEP, STEP)
+                    out_ref[s, pl.ds(at, STEP), :] = value[
+                        rows, t * LANES : (t + 1) * LANES
+                    ].astype(jnp.bfloat16)
+                turned = pltpu.roll(value[rows, tiles * LANES :], QUARTER * (a // 2), 1)
+                ends_ref[s, pl.ds(spot, STEP), :] = jnp.where(
+                    group_lane == a // 2, turned, ends_ref[s, pl.ds(spot, STEP), :]
+                )
+
+        @pl.when(used)
+        def _():
+            down = sum_refs[0][a].astype(jnp.float32)
+            for ref in sum_refs[1:]:
+                down = down + ref[a].astype(jnp.float32)
+            down = down.astype(jnp.bfloat16).astype(jnp.float32)
+            turned = pltpu.roll(down, HALF, 1)
+            twice = jnp.concatenate(
+                [jnp.where(low, down, turned), jnp.where(low, turned, down)], axis=0
             )
-            first = first_ref[k].astype(jnp.float32)
-            for t in range(weight_ref.shape[0] // LANES):
-                columns = slice(t * LANES, (t + 1) * LANES)
-                picked = jnp.where(label == first + 2.0 * t, product[:, columns], picked)
-        picked = picked + pltpu.roll(picked, HALF, 1)
-        out_ref[c] = jnp.where(low, picked[0 : 2 * cap], picked[2 * cap :]).astype(jnp.bfloat16)
+            delta = jnp.zeros((senders * STEP, width), jnp.float32)
+            for k, weight in enumerate(weight_blocks(near_refs, opened_ref)):
+                first = first_ref[k].astype(jnp.float32)
+                placed = [
+                    jnp.where(lowered == first + 2.0 * t, twice, 0.0)
+                    for t in range(weight.shape[0] // LANES)
+                ]
+                placed = jnp.concatenate(placed, axis=1).astype(jnp.bfloat16)
+                delta = delta + jnp.dot(placed, weight, preferred_element_type=jnp.float32)
+            leave(delta)
+
+        @pl.when(jnp.logical_not(used))
+        def _():
+            leave(jnp.zeros((senders * STEP, width), jnp.float32))
+
         return carry
 
-    lax.fori_loop(0, senders // 4, one, 0)
-
-
-def up_kernel(first_ref, rows_ref, *refs):
-    sum_refs, weight_refs, out_ref = refs[:QUAD], refs[QUAD:-1], refs[-1]
-    senders, cap, width = rows_ref.shape
-    kept = out_ref.shape[1]
-    low = lanes_of(2 * cap) < HALF
-
-    def one(c, carry):
-        down = sum_refs[0][c].astype(jnp.float32)
-        for ref in sum_refs[1:]:
-            down = down + ref[c].astype(jnp.float32)
-        down = down.astype(jnp.bfloat16).astype(jnp.float32)
-        turned = pltpu.roll(down, HALF, 1)
-        pairs = [jnp.where(low, down, turned), jnp.where(low, turned, down)]
-        twice = jnp.concatenate(
-            [pairs[i // 2][i % 2 * cap : i % 2 * cap + kept] for i in range(4)], axis=0
-        )
-        ends = [rows_ref[4 * c + i, 0:kept, width - LANES :] for i in range(4)]
-        label = label_of(jnp.concatenate(ends, axis=0))
-        delta = jnp.zeros((4 * kept, width), jnp.float32)
-        for k, weight_ref in enumerate(weight_refs):
-            first = first_ref[k].astype(jnp.float32)
-            placed = [
-                jnp.where(label == first + 2.0 * t, twice, 0.0)
-                for t in range(weight_ref.shape[0] // LANES)
-            ]
-            placed = jnp.concatenate(placed, axis=1).astype(jnp.bfloat16)
-            delta = delta + jnp.dot(placed, weight_ref[...], preferred_element_type=jnp.float32)
-        for i in range(4):
-            out_ref[4 * c + i] = delta[i * kept : (i + 1) * kept].astype(jnp.bfloat16)
-        return carry
-
-    lax.fori_loop(0, senders // 4, one, 0)
+    lax.fori_loop(0, kept // STEP, one, 0)
+    for s in range(senders):
+        out_ref[s, tiles * kept :, :] = ends_ref[s].astype(jnp.bfloat16)
 
 
 def mix_kernel(whole, target_ref, tokens_ref, returned_ref, out_ref):
     total = tokens_ref.shape[0]
-    quads, cap = returned_ref.shape[0] // QUAD, returned_ref.shape[1]
-    quarter = LANES // QUAD
+    tiles = whole // LANES
+    quads, kept = returned_ref.shape[0] // QUAD, (returned_ref.shape[1] - QUARTER) // tiles
     lane = lanes_of(total)
-    spot = lax.broadcasted_iota(jnp.int32, (total, quads * cap), 1)
-    place = spot // cap * total + spot % cap
+    spot = lax.broadcasted_iota(jnp.int32, (total, quads * kept), 1)
+    place = spot // kept * total + spot % kept
     chosen = jnp.where(target_ref[...] == place, 1.0, 0.0).astype(jnp.bfloat16)
     end = jnp.zeros((total, LANES), jnp.float32)
     for j in range(QUAD):
-        share = jnp.concatenate([returned_ref[q * QUAD + j] for q in range(quads)], axis=0)
+        shares = []
+        for q in range(quads):
+            d = q * QUAD + j
+            parts = [returned_ref[d, t * kept : (t + 1) * kept, :] for t in range(tiles)]
+            packed = returned_ref[d, tiles * kept :, :].astype(jnp.float32)
+            groups = [packed]
+            for m in range(1, QUAD):
+                groups.append(pltpu.roll(packed, LANES - QUARTER * m, 1))
+            parts.append(jnp.concatenate(groups, axis=0)[0:kept].astype(jnp.bfloat16))
+            shares.append(jnp.concatenate(parts, axis=1))
+        share = jnp.concatenate(shares, axis=0)
         delta = jnp.dot(chosen, share, preferred_element_type=jnp.float32)
         columns = slice(j * whole, (j + 1) * whole)
         out_ref[:, columns] = (
             tokens_ref[:, columns].astype(jnp.float32) + delta[:, 0:whole]
         ).astype(jnp.bfloat16)
         last = delta[:, whole:]
-        turned = pltpu.roll(last, quarter * j, 1) if j else last
-        end = jnp.where((lane >= quarter * j) & (lane < quarter * (j + 1)), turned, end)
+        turned = pltpu.roll(last, QUARTER * j, 1) if j else last
+        end = jnp.where((lane >= QUARTER * j) & (lane < QUARTER * (j + 1)), turned, end)
     out_ref[:, QUAD * whole :] = (
         tokens_ref[:, QUAD * whole :].astype(jnp.float32) + end
     ).astype(jnp.bfloat16)
@@ -241,22 +360,25 @@
     return lax.ppermute(value, "groups", [(0, 1), (1, 0)])
 
 
-def back_and_mix(
-    kept, tokens, target, first, arrived, sums, up_weights, *unused_values
-):
+def back_and_mix(kept, tokens, target, first, arrived, sums, up_weights, *unused_values):
     blocks, rows, width = tokens.shape
     total = blocks * rows
-    devices, cap, share = arrived.shape
-    columns = sum(weight.shape[0] for weight in up_weights)
+    devices = arrived.shape[0]
+    columns, share = up_weights[0].shape
+    whole = share - LANES
     leaving = call(
         up_kernel,
-        jax.ShapeDtypeStruct((devices, kept, share), jnp.bfloat16),
+        jax.ShapeDtypeStruct((devices, whole // LANES * kept + QUARTER, LANES), jnp.bfloat16),
         [SMEM] + [VMEM] * (1 + QUAD + len(up_weights)),
-        2 * devices * kept * columns * share,
-        2 * (2 * devices * kept + columns) * share,
+        2 * devices * kept * QUAD * columns * share,
+        2 * (2 * devices * kept + QUAD * columns) * share,
+        scratch=[
+            pltpu.VMEM((4, columns // 2, share), jnp.bfloat16),
+            pltpu.VMEM((devices, QUARTER, LANES), jnp.float32),
+        ],
     )(first, arrived, *sums, *up_weights)
     mixed = call(
-        functools.partial(mix_kernel, share - LANES),
+        functools.partial(mix_kernel, whole),
         jax.ShapeDtypeStruct((total, width), jnp.bfloat16),
         [VMEM] * 3,
         2 * devices * kept * total * share,
@@ -287,7 +409,8 @@
     same = quad[:, None] == quad[None, :]
     used = request_block_rows
     ahead = jnp.where(same & (serial[None, :] < serial[:, None]), used[None, :], 0)
-    most = jnp.max(jnp.sum(jnp.where(same, used[None, :], 0), axis=1))
+    most = jnp.max(jnp.sum(jnp.where(same, used[None, :], 0), axis=1)).astype(jnp.float32)
+    most = jnp.maximum(most, swapped(most.reshape(1, 1))[0, 0]).astype(i32)
     row = jnp.arange(rows, dtype=i32)
     start = quad * total + jnp.sum(ahead, axis=1)
     target = jnp.where(row[None, :] < used[:, None], start[:, None] + row[None, :], -1)
@@ -303,13 +426,13 @@
         + [parts[2:] * resident + twin_half]
     ).astype(i32)
 
+    tiles = whole // LANES
+
     def shares(weight, which, after):
+        far = (columns // 2 * tiles + columns // 2 // QUAD, LANES)
         values = call(
             functools.partial(weight_kernel, whole, which),
-            [
-                jax.ShapeDtypeStruct((columns if k < 2 else columns // 2, share), bf16)
-                for k in which
-            ],
+            [jax.ShapeDtypeStruct((columns, share) if k < 2 else far, bf16) for k in which],
             [SMEM, SMEM, VMEM],
             0,
             len(which) * columns * width,
@@ -326,12 +449,13 @@
     down_weights.append(swapped(down_weights[3]))
     up_weights.append(swapped(up_weights[2]))
     up_weights.append(swapped(up_weights[3]))
+
     caps = [total * 5 // 16, total * 6 // 16, total * 7 // 16]
     cap = caps[-1]
     arrived = exchange(
         call(
-            functools.partial(pack_kernel, whole),
-            jax.ShapeDtypeStruct((devices, cap, share), bf16),
+            functools.partial(pack_kernel, whole, cap),
+            jax.ShapeDtypeStruct((devices, tiles * cap + QUARTER, LANES), bf16),
             [SMEM, VMEM, VMEM, VMEM],
             2 * devices * cap * total * share,
             2 * (total * width + devices * cap * share),
@@ -339,16 +463,19 @@
         )(most.reshape(1), target.reshape(1, total), label, tokens.reshape(total, width))
     )
 
-    most = jnp.max(arrived[:, 0, whole + LANES // QUAD + 1].astype(jnp.float32)).reshape(1, 1)
-    others_most = swapped(most)
-    most = jnp.maximum(most, others_most)[0, 0].astype(i32)
+    counts = arrived[:, tiles * cap + STEP, NOTE + cap // STEP].astype(jnp.float32)
+    most = jnp.max(counts).astype(i32)
     partial = call(
         down_kernel,
-        jax.ShapeDtypeStruct((devices // 4, 2 * cap, LANES), bf16),
+        jax.ShapeDtypeStruct((cap // STEP, devices * STEP // 2, LANES), bf16),
         [SMEM] + [VMEM] * (1 + len(down_weights)),
-        2 * devices * cap * 4 * columns * share,
-        2 * (devices * cap + 4 * columns) * share,
-        [up_weights[4], others_most],
+        2 * devices * cap * QUAD * columns * share,
+        2 * (devices * cap + QUAD * columns) * share,
+        up_weights[4:5],
+        [
+            pltpu.VMEM((4, columns // 2, share), bf16),
+            pltpu.VMEM((devices * STEP, share), bf16),
+        ],
     )(first, arrived, *down_weights)
     sums = [partial] + [towards(partial, k, devices) for k in range(1, QUAD)]
     return lax.switch(
@@ -382,6 +509,7 @@
         slots = max(1, 4 * blocks // devices)
         quads = devices % QUAD == 0 and slots * QUAD >= blocks
         quads = quads and width % (QUAD * LANES) == LANES and up_weight.shape[1] == HALF
+        quads = quads and blocks * rows * 7 // 16 == 7 * STEP and mesh.shape["groups"] == 2
         plan = rows_to_quads if quads else rows_to_holders
         return plan(tokens, request_block_adapter, request_block_rows, down_weight, up_weight)
 

time: 202 us -> 194 us (0.960); the launches traced: 202 us -> 191 us
  starting transfers between devices: 36.4 us -> 27 us
  waiting for transfers between devices: 118 us -> 114 us
  Pallas kernels: 35.9 us -> 39.8 us
    ppermute x9, waiting for transfers between devices: 65.7 us -> 58.3 us  [towards(): return lax.ppermute(value, 'adapter', [(i, i ^ k) for i in range(devices)])]
    ppermute x5, starting transfers between devices: 12.7 us -> 5.66 us  [swapped(): return lax.ppermute(value, 'groups', [(0, 1), (1, 0)])]
    all_to_all x2, waiting for transfers between devices: 51.5 us -> 55.7 us  [exchange(): lax.all_to_all(value, 'adapter', split_axis=0, concat_axis=0, tiled=True)]
    pallas_call x4, Pallas kernels: 28.8 us -> 31.4 us  [the longest x1 11.9 us: rows_to_quads(): call(down_kernel, jax.ShapeDtypeStruct((cap // STEP, devices * STEP // 2,...]
    ppermute x9, starting transfers between devices: 10.7 us -> 8.59 us  [towards(): return lax.ppermute(value, 'adapter', [(i, i ^ k) for i in range(devices)])]
  transfers between devices with their start and end apart: 16 -> 16, of which waited for: 8 -> 7; matrix products, arithmetic and copies ran while one was open for 1% -> 1% of each run, Pallas kernels for 9% -> 11%
where the time goes in v2:
time: 194 us; the launch traced here: 191 us
  waiting for transfers between devices  114 us (59%)
  Pallas kernels  39.8 us (21%)
  starting transfers between devices  27 us (14%)
  other arithmetic  4.59 us (2%)
  local copies, waits for them, and re-layouts  3.12 us (2%)
  between operations  2.03 us (1%)
    ppermute x9, waiting for transfers between devices, towards(): return lax.ppermute(value, 'adapter', [(i, i ^ k) for i in range(devices)])  58.3 us
    all_to_all x2, waiting for transfers between devices, exchange(): lax.all_to_all(value, 'adapter', split_axis=0, concat_axis=0, tiled=True)  55.7 us
    all_to_all x2, starting transfers between devices, exchange(): lax.all_to_all(value, 'adapter', split_axis=0, concat_axis=0, tiled=True)  12.8 us
    pallas_call x1, Pallas kernels, rows_to_quads(): call(down_kernel, jax.ShapeDtypeStruct((cap // STEP, devices * STEP // 2,...  11.9 us
    pallas_call x1, Pallas kernels, back_and_mix(): call(up_kernel, jax.ShapeDtypeStruct((devices, whole // LANES * kept + QU...  11.9 us
    ppermute x9, starting transfers between devices, towards(): return lax.ppermute(value, 'adapter', [(i, i ^ k) for i in range(devices)])  8.59 us
    pallas_call x3, Pallas kernels, shares(): call(functools.partial(weight_kernel, whole, which), [jax.ShapeDtypeStruc...  8.45 us
    ppermute x5, starting transfers between devices, swapped(): return lax.ppermute(value, 'groups', [(0, 1), (1, 0)])  5.66 us
  transfers between devices with their start and end apart: 16, of which 7 were waited for; matrix products, arithmetic and copies ran while one was open for 1% of the time, Pallas kernels for 11%

profile of v2, /device:TPU:11, one launch (start us, length us, event | category | flops | bytes accessed | tf_op | source)
XLA Modules:
  0.0 190.8 jit_solution(17319284510729471765)
XLA Ops:
  2.8 2.0 %collective-permute-start = (f32[1,1]{1,0:T(1,128)}, f32[1,1]{1,0:T(1,128)}, u32[]{:S(2)}, u32[]{:S(2)}) collective-permute-start(f32[1,1]{1,0:T(1,128)} %bitcast.14), channel_id=1, source_target_pairs={{0,16},{16,0},{1,17},{17,1},{2,18},{18,2},{3,19},{19,3},{4,20},{20... | collective-permute-start | bytes 20 | tf_op jit(solution)/shard_map/ppermute | solution.py:360
  6.5 4.9 %shard_map.59 = bf16[16,704,128]{2,1,0:T(8,128)(2,1)} custom-call(s32[1]{0:T(128)} %bitcast.16.most_ref, s32[1,256]{1,0:T(1,128)S(1)} %select_n.72.target_ref, f32[256,1]{1,0:T(8,128)S(1)} %convert_element_type.53.label_ref, bf16[256,3200]{1,0:T(8,128)(2,1)} %bitcast.29), custom_call_target="tpu_custom_call" | custom-call | flops 822083584 | bytes 4849664 | tf_op jit(solution)/shard_map/pallas_call | solution.py:456
  11.3 7.4 %all-to-all-start.6 = ((bf16[16,704,128]{2,1,0:T(8,128)(2,1)}), bf16[16,704,128]{2,1,0:T(8,128)(2,1)}, u32[]{:S(2)}, u32[]{:S(2)}) async-start(bf16[16,704,128]{2,1,0:T(8,128)(2,1)} %shard_map.59), calls=%async_computation.6 | async-start | bytes 5767168 | tf_op jit(solution)/shard_map/all_to_all | solution.py:352
  18.7 3.2 %shard_map.60 = (bf16[512,896]{1,0:T(8,128)(2,1)S(1)}, bf16[512,896]{1,0:T(8,128)(2,1)}, bf16[1600,128]{1,0:T(8,128)(2,1)S(1)}, bf16[1600,128]{1,0:T(8,128)(2,1)S(1)}) custom-call(s32[4]{0:T(128)S(1)} %iota_xor_fusion.part_ref.refs_1_.refs_2_, s32[1]{0:T(128)} %bitcast.19.group_ref.refs_2_.refs_3_, bf16[512,3200]{1,0:T(8,128)(2,1)} %bitcast.37), custom_call_target="tpu_custom_call" | custom-call | bytes 6553600 | tf_op jit(solution)/shard_map/pallas_call | solution.py:433
  23.9 20.3 %collective-permute-done.1.refs_0_.refs_5_ = bf16[1600,128]{1,0:T(8,128)(2,1)S(1)} collective-permute-done((bf16[1600,128]{1,0:T(8,128)(2,1)S(1)}, bf16[1600,128]{1,0:T(8,128)(2,1)S(1)}, u32[]{:S(2)}, u32[]{:S(2)}) %collective-permute-start.1) | collective-permute-done | bytes 409632 | tf_op jit(solution)/shard_map/ppermute | solution.py:356
  45.1 3.2 %shard_map.61 = (bf16[512,896]{1,0:T(8,128)(2,1)}, bf16[512,896]{1,0:T(8,128)(2,1)S(1)}, bf16[1600,128]{1,0:T(8,128)(2,1)}) custom-call(bf16[1600,128]{1,0:T(8,128)(2,1)S(1)} %collective-permute-done.1.refs_0_.refs_5_, s32[4]{0:T(128)S(1)} %iota_xor_fusion.part_ref.refs_1_.refs_2_, s32[1]{0:T(128)} %bitcast.19.group_ref.refs_2_.refs_3_, ...), custom_call_target="tpu_custom_call" | custom-call | bytes 4915200 | tf_op jit(solution)/shard_map/pallas_call | solution.py:433
  48.3 2.3 %collective-permute-start.2 = (bf16[1600,128]{1,0:T(8,128)(2,1)}, bf16[1600,128]{1,0:T(8,128)(2,1)}, u32[]{:S(2)}, u32[]{:S(2)}) collective-permute-start(bf16[1600,128]{1,0:T(8,128)(2,1)} %get-tuple-element.201), channel_id=1, source_target_pairs={{0,2},{1,3},{2,0},{3,1},{4,6},{5,7},{6,4},{7,5},{8,10},{9,11},{10,... | collective-permute-start | bytes 1228808 | tf_op jit(solution)/shard_map/ppermute | solution.py:356
  50.6 11.1 %collective-permute-done.5.refs_6_.refs_0_ = bf16[1600,128]{1,0:T(8,128)(2,1)S(1)} collective-permute-done((bf16[1600,128]{1,0:T(8,128)(2,1)S(1)}, bf16[1600,128]{1,0:T(8,128)(2,1)S(1)}, u32[]{:S(2)}, u32[]{:S(2)}) %collective-permute-start.5) | collective-permute-done | bytes 409632 | tf_op jit(solution)/shard_map/ppermute | solution.py:356
  62.6 2.1 %shard_map.63 = bf16[1600,128]{1,0:T(8,128)(2,1)S(1)} custom-call(bf16[1600,128]{1,0:T(8,128)(2,1)S(1)} %collective-permute-done.5.refs_6_.refs_0_, bf16[1600,128]{1,0:T(8,128)(2,1)S(1)} %collective-permute-done.6.refs_7_.refs_1_, s32[4]{0:T(128)S(1)} %iota_xor_fusion.part_ref.refs_1_.refs_2_, s32[1]{0:T(128)} %bitcast.19.group_ref.refs_2_.refs_3_, ...), custom_call_target="tpu_custom_call" | custom-call | bytes 1638400 | tf_op jit(solution)/shard_map/pallas_call | solution.py:433
  65.5 7.9 %collective-permute-done.2 = bf16[1600,128]{1,0:T(8,128)(2,1)} collective-permute-done((bf16[1600,128]{1,0:T(8,128)(2,1)}, bf16[1600,128]{1,0:T(8,128)(2,1)}, u32[]{:S(2)}, u32[]{:S(2)}) %collective-permute-start.2) | collective-permute-done | bytes 409632 | tf_op jit(solution)/shard_map/ppermute | solution.py:356
  74.5 1.6 collective-permute-start.11
  76.2 10.1 %collective-permute-done.12 = bf16[1600,128]{1,0:T(8,128)(2,1)} collective-permute-done((bf16[1600,128]{1,0:T(8,128)(2,1)S(1)}, bf16[1600,128]{1,0:T(8,128)(2,1)}, u32[]{:S(2)}, u32[]{:S(2)}) %collective-permute-start.12) | collective-permute-done | bytes 409632 | tf_op jit(solution)/shard_map/ppermute | solution.py:356
  87.2 11.9 %shard_map.62 = bf16[7,128,128]{2,1,0:T(8,128)(2,1)} custom-call(bf16[1600,128]{1,0:T(8,128)(2,1)} %collective-permute-done.3.refs_0_, s32[6]{0:T(128)S(1)} %pad_add_fusion.refs_1_, bf16[16,704,128]{2,1,0:T(8,128)(2,1)} %all-to-all-done.6.refs_2_, bf16[512,896]{1,0:T(8,128)(2,1)S(1)} %get-tuple-element.202.refs_3_, ...), custom_call_target="tpu_custom_call" | custom-call | flops 6576668672 | bytes 6881280 | tf_op jit(solution)/shard_map/pallas_call | solution.py:468
  99.1 1.6 collective-permute-start.10
  101.0 1.5 slice_reduce_fusion
  103.1 4.1 %collective-permute-done.10 = bf16[7,128,128]{2,1,0:T(8,128)(2,1)S(1)} collective-permute-done((bf16[7,128,128]{2,1,0:T(8,128)(2,1)}, bf16[7,128,128]{2,1,0:T(8,128)(2,1)S(1)}, u32[]{:S(2)}, u32[]{:S(2)}) %collective-permute-start.10) | collective-permute-done | bytes 229408 | tf_op jit(solution)/shard_map/ppermute | solution.py:356
  107.2 4.8 %collective-permute-done.9 = bf16[7,128,128]{2,1,0:T(8,128)(2,1)S(1)} collective-permute-done((bf16[7,128,128]{2,1,0:T(8,128)(2,1)}, bf16[7,128,128]{2,1,0:T(8,128)(2,1)S(1)}, u32[]{:S(2)}, u32[]{:S(2)}) %collective-permute-start.9) | collective-permute-done | bytes 229408 | tf_op jit(solution)/shard_map/ppermute | solution.py:356
  112.2 77.5 %conditional.1 = (bf16[32,8,3200]{2,1,0:T(8,128)(2,1)S(1)}) conditional(s32[]{:T(128)} %clamp.3, (s32[32,8]{1,0:T(8,128)S(1)}, s32[32,8]{1,0:T(8,128)S(1)}, s32[32,8]{1,0:T(8,128)S(1)}, s32[32,8]{1,0:T(8,128)S(1)}, bf16[32,8,3200]{2,1,0:T(8,128)(2,1)}, /*index=5*/s32[6]{0:T(128)S(1)}, ...), branch_computations={%region_4.5_spmd, %region_5.6_spmd, %region_6.7_spmd, %region_7.12... | conditional | flops 7398753280 | bytes 107581608 | solution.py:481
  112.2 11.9 %branch_1_fun.2 = bf16[16,608,128]{2,1,0:T(8,128)(2,1)S(1)} custom-call(s32[6]{0:T(128)S(1)} %get-tuple-element.159.first_ref, bf16[16,704,128]{2,1,0:T(8,128)(2,1)} %get-tuple-element.160.rows_ref, bf16[7,128,128]{2,1,0:T(8,128)(2,1)} %get-tuple-element.161.refs_0_, bf16[7,128,128]{2,1,0:T(8,128)(2,1)S(1)} %get-tuple-element.162.refs_1_, ...), custom_call_target="tpu_custom_call" | custom-call | flops 5637144576 | bytes 9175040 | tf_op jit(solution)/shard_map/cond/branch_1_fun/pallas_call | solution.py:369
  124.1 1.5 copy-done.1
  125.6 5.3 %all-to-all-start.1 = ((bf16[16,608,128]{2,1,0:T(8,128)(2,1)}), bf16[16,608,128]{2,1,0:T(8,128)(2,1)S(1)}, u32[]{:S(2)}, u32[]{:S(2)}) async-start(bf16[16,608,128]{2,1,0:T(8,128)(2,1)} %copy-done.1), calls=%async_computation.1 | async-start | bytes 4980736 | tf_op jit(solution)/shard_map/cond/branch_1_fun/all_to_all | solution.py:352
  131.0 55.7 %all-to-all-done.1.returned_ref = bf16[16,608,128]{2,1,0:T(8,128)(2,1)S(1)} async-done(((bf16[16,608,128]{2,1,0:T(8,128)(2,1)}), bf16[16,608,128]{2,1,0:T(8,128)(2,1)S(1)}, u32[]{:S(2)}, u32[]{:S(2)}) %all-to-all-start.1) | async-done | bytes 2490400 | tf_op jit(solution)/shard_map/cond/branch_1_fun/all_to_all | solution.py:352
  186.7 2.7 %branch_1_fun.3 = bf16[256,3200]{1,0:T(8,128)(2,1)S(1)} custom-call(s32[256,1]{1,0:T(8,128)S(1)} %reshape_reshape.11.target_ref, bf16[256,3200]{1,0:T(8,128)(2,1)} %bitcast.31, bf16[16,608,128]{2,1,0:T(8,128)(2,1)S(1)} %all-to-all-done.1.returned_ref), custom_call_target="tpu_custom_call" | custom-call | flops 704643072 | bytes 6029312 | tf_op jit(solution)/shard_map/cond/branch_1_fun/pallas_call | solution.py:380
  189.7 1.2 copy-done.5
  (43 shorter events, 10.4 us)
Async XLA Ops:
  2.8 3.0 %collective-permute-start = (f32[1,1]{1,0:T(1,128)}, f32[1,1]{1,0:T(1,128)}, u32[]{:S(2)}, u32[]{:S(2)}) collective-permute-start(f32[1,1]{1,0:T(1,128)} %bitcast.14), channel_id=1, source_target_pairs={{0,16},{16,0},{1,17},{17,1},{2,18},{18,2},{3,19},{19,3},{4,20},{20... | collective-permute-start | bytes 20 | tf_op jit(solution)/shard_map/ppermute | solution.py:360
  11.3 75.9 %all-to-all-start.6 = ((bf16[16,704,128]{2,1,0:T(8,128)(2,1)}), bf16[16,704,128]{2,1,0:T(8,128)(2,1)}, u32[]{:S(2)}, u32[]{:S(2)}) async-start(bf16[16,704,128]{2,1,0:T(8,128)(2,1)} %shard_map.59), calls=%async_computation.6 | async-start | bytes 5767168 | tf_op jit(solution)/shard_map/all_to_all | solution.py:352
  21.9 22.3 %collective-permute-start.1 = (bf16[1600,128]{1,0:T(8,128)(2,1)S(1)}, bf16[1600,128]{1,0:T(8,128)(2,1)S(1)}, u32[]{:S(2)}, u32[]{:S(2)}) collective-permute-start(bf16[1600,128]{1,0:T(8,128)(2,1)S(1)} %get-tuple-element.200), channel_id=1, source_target_pairs={{0,2},{1,3},{2,0},{3,1},{4,6},{5,7},{6,4},{7,5},{8,10},{9,11},{10,... | collective-permute-start | bytes 1228808 | tf_op jit(solution)/shard_map/ppermute | solution.py:356
  22.2 65.0 %collective-permute-start.4 = (bf16[512,896]{1,0:T(8,128)(2,1)}, bf16[512,896]{1,0:T(8,128)(2,1)}, u32[]{:S(2)}, u32[]{:S(2)}) collective-permute-start(bf16[512,896]{1,0:T(8,128)(2,1)} %get-tuple-element.203), channel_id=1, source_target_pairs={{0,1},{1,0},{2,3},{3,2},{4,5},{5,4},{6,7},{7,6},{8,9},{9,8},{10,11... | collective-permute-start | bytes 2752520 | tf_op jit(solution)/shard_map/ppermute | solution.py:356
  22.8 38.9 %collective-permute-start.5 = (bf16[1600,128]{1,0:T(8,128)(2,1)S(1)}, bf16[1600,128]{1,0:T(8,128)(2,1)S(1)}, u32[]{:S(2)}, u32[]{:S(2)}) collective-permute-start(bf16[1600,128]{1,0:T(8,128)(2,1)S(1)} %get-tuple-element.204), channel_id=1, source_target_pairs={{0,3},{1,2},{2,1},{3,0},{4,7},{5,6},{6,5},{7,4},{8,11},{9,10},{10,... | collective-permute-start | bytes 1228808 | tf_op jit(solution)/shard_map/ppermute | solution.py:356
  44.2 18.4 %collective-permute-start.6 = (bf16[1600,128]{1,0:T(8,128)(2,1)S(1)}, bf16[1600,128]{1,0:T(8,128)(2,1)S(1)}, u32[]{:S(2)}, u32[]{:S(2)}) collective-permute-start(bf16[1600,128]{1,0:T(8,128)(2,1)S(1)} %collective-permute-done.1.refs_0_.refs_5_), channel_id=1, source_target_pairs={{0,16},{16,0},{1,17},{17,1},{2,18},{18,2},{3,19},{19,3},{4,20},{20... | collective-permute-start | bytes 1228808 | tf_op jit(solution)/shard_map/ppermute | solution.py:360
  48.3 25.1 %collective-permute-start.2 = (bf16[1600,128]{1,0:T(8,128)(2,1)}, bf16[1600,128]{1,0:T(8,128)(2,1)}, u32[]{:S(2)}, u32[]{:S(2)}) collective-permute-start(bf16[1600,128]{1,0:T(8,128)(2,1)} %get-tuple-element.201), channel_id=1, source_target_pairs={{0,2},{1,3},{2,0},{3,1},{4,6},{5,7},{6,4},{7,5},{8,10},{9,11},{10,... | collective-permute-start | bytes 1228808 | tf_op jit(solution)/shard_map/ppermute | solution.py:356
  61.7 25.5 %collective-permute-start.7 = (bf16[1600,128]{1,0:T(8,128)(2,1)S(1)}, bf16[1600,128]{1,0:T(8,128)(2,1)S(1)}, u32[]{:S(2)}, u32[]{:S(2)}) collective-permute-start(bf16[1600,128]{1,0:T(8,128)(2,1)S(1)} %collective-permute-done.5.refs_6_.refs_0_), channel_id=1, source_target_pairs={{0,16},{16,0},{1,17},{17,1},{2,18},{18,2},{3,19},{19,3},{4,20},{20... | collective-permute-start | bytes 1228808 | tf_op jit(solution)/shard_map/ppermute | solution.py:360
  64.7 21.6 %collective-permute-start.12 = (bf16[1600,128]{1,0:T(8,128)(2,1)S(1)}, bf16[1600,128]{1,0:T(8,128)(2,1)}, u32[]{:S(2)}, u32[]{:S(2)}) collective-permute-start(bf16[1600,128]{1,0:T(8,128)(2,1)S(1)} %shard_map.63), channel_id=1, source_target_pairs={{0,3},{1,2},{2,1},{3,0},{4,7},{5,6},{6,5},{7,4},{8,11},{9,10},{10,... | collective-permute-start | bytes 1228808 | tf_op jit(solution)/shard_map/ppermute | solution.py:356
  73.5 13.7 %collective-permute-start.3 = (bf16[1600,128]{1,0:T(8,128)(2,1)}, bf16[1600,128]{1,0:T(8,128)(2,1)}, u32[]{:S(2)}, u32[]{:S(2)}) collective-permute-start(bf16[1600,128]{1,0:T(8,128)(2,1)} %collective-permute-done.2), channel_id=1, source_target_pairs={{0,16},{16,0},{1,17},{17,1},{2,18},{18,2},{3,19},{19,3},{4,20},{20... | collective-permute-start | bytes 1228808 | tf_op jit(solution)/shard_map/ppermute | solution.py:360
  74.5 28.6 %collective-permute-start.11 = (bf16[512,896]{1,0:T(8,128)(2,1)S(1)}, bf16[512,896]{1,0:T(8,128)(2,1)}, u32[]{:S(2)}, u32[]{:S(2)}) collective-permute-start(bf16[512,896]{1,0:T(8,128)(2,1)S(1)} %get-tuple-element.206), channel_id=1, source_target_pairs={{0,1},{1,0},{2,3},{3,2},{4,5},{5,4},{6,7},{7,6},{8,9},{9,8},{10,11... | collective-permute-start | bytes 2752520 | tf_op jit(solution)/shard_map/ppermute | solution.py:356
  86.3 16.9 %collective-permute-start.13 = (bf16[1600,128]{1,0:T(8,128)(2,1)}, bf16[1600,128]{1,0:T(8,128)(2,1)}, u32[]{:S(2)}, u32[]{:S(2)}) collective-permute-start(bf16[1600,128]{1,0:T(8,128)(2,1)} %collective-permute-done.12), channel_id=1, source_target_pairs={{0,16},{16,0},{1,17},{17,1},{2,18},{18,2},{3,19},{19,3},{4,20},{20... | collective-permute-start | bytes 1228808 | tf_op jit(solution)/shard_map/ppermute | solution.py:360
  87.2 24.9 %copy-start.6 = (s32[32]{0:T(128)S(1)}, s32[32]{0:T(128)}, u32[]{:S(2)}) copy-start(s32[32]{0:T(128)} %param.11) | copy-start | bytes 388
  87.2 25.0 %copy-start.7 = (s32[32]{0:T(128)S(1)}, s32[32]{0:T(128)}, u32[]{:S(2)}) copy-start(s32[32]{0:T(128)} %param.10) | copy-start | bytes 388
  99.1 8.1 %collective-permute-start.10 = (bf16[7,128,128]{2,1,0:T(8,128)(2,1)}, bf16[7,128,128]{2,1,0:T(8,128)(2,1)S(1)}, u32[]{:S(2)}, u32[]{:S(2)}) collective-permute-start(bf16[7,128,128]{2,1,0:T(8,128)(2,1)} %shard_map.62), channel_id=1, source_target_pairs={{0,3},{1,2},{2,1},{3,0},{4,7},{5,6},{6,5},{7,4},{8,11},{9,10},{10,... | collective-permute-start | bytes 688136 | tf_op jit(solution)/shard_map/ppermute | solution.py:356
  100.7 6.6 %collective-permute-start.8 = (bf16[7,128,128]{2,1,0:T(8,128)(2,1)}, bf16[7,128,128]{2,1,0:T(8,128)(2,1)S(1)}, u32[]{:S(2)}, u32[]{:S(2)}) collective-permute-start(bf16[7,128,128]{2,1,0:T(8,128)(2,1)} %shard_map.62), channel_id=1, source_target_pairs={{0,1},{1,0},{2,3},{3,2},{4,5},{5,4},{6,7},{7,6},{8,9},{9,8},{10,11... | collective-permute-start | bytes 688136 | tf_op jit(solution)/shard_map/ppermute | solution.py:356
  100.7 11.3 %collective-permute-start.9 = (bf16[7,128,128]{2,1,0:T(8,128)(2,1)}, bf16[7,128,128]{2,1,0:T(8,128)(2,1)S(1)}, u32[]{:S(2)}, u32[]{:S(2)}) collective-permute-start(bf16[7,128,128]{2,1,0:T(8,128)(2,1)} %shard_map.62), channel_id=1, source_target_pairs={{0,2},{1,3},{2,0},{3,1},{4,6},{5,7},{6,4},{7,5},{8,10},{9,11},{10,... | collective-permute-start | bytes 688136 | tf_op jit(solution)/shard_map/ppermute | solution.py:356
  124.1 1.5 copy-start.1
  125.6 61.2 %all-to-all-start.1 = ((bf16[16,608,128]{2,1,0:T(8,128)(2,1)}), bf16[16,608,128]{2,1,0:T(8,128)(2,1)S(1)}, u32[]{:S(2)}, u32[]{:S(2)}) async-start(bf16[16,608,128]{2,1,0:T(8,128)(2,1)} %copy-done.1), calls=%async_computation.1 | async-start | bytes 4980736 | tf_op jit(solution)/shard_map/cond/branch_1_fun/all_to_all | solution.py:352
  189.7 1.2 copy-start.5
